TPU v7x, 128 devices: a whole 4x4x4 slice. The times are simulated.
128 devices in a mesh: member: 8 (over z, y_lo), row: 16 (over y_hi, x, core).
Axes of the slice: x: 4, y: 4 (y_hi: 2, y_lo: 2; y = y_hi * 2 + y_lo), z: 4, core: 2. Of those that a mesh axis runs over, the one named last changes fastest.
Arguments:
- action: bfloat16 [4096, 1024], P('row'), may hold values from -6 to 6
- state_term: bfloat16 [16, 4096, 4096], P('member', 'row'), may hold values from -6 to 6
- target: float32 [4096], P('row'), may hold values from -6 to 6
- weight_a: bfloat16 [16, 1024, 4096], P('member', 'row'), may hold values from -0.21875 to 0.21875
- value_w: bfloat16 [16, 4096], P('member'), may hold values from -0.0234375 to 0.0234375
Outputs:
- weight_grad: bfloat16 [16, 1024, 4096], P('member', 'row')
- value_grad: float32 [16, 4096], P('member')
- state_grad: bfloat16 [16, 4096, 4096], P('member', 'row')
- diversity: float32 [4096], P('row')
All inputs are finite; a program needn't handle non-finite values.
Results may differ from a plain program's by a relative error of at most 0.03.
Values may be sent and summed in bfloat16 or wider, within the bound.
A program may use at most 128 MiB of HBM per device.

v0:
```python
import jax
import jax.numpy as jnp
from jax import lax
from jax.sharding import PartitionSpec as P

EPS = 1e-06
ETA = 5.0


def forward_member(weights, value_row, state_rows, action):
    pre_act = state_rows.astype(jnp.float32) + jnp.dot(
        action, weights, preferred_element_type=jnp.float32
    )
    sigmoid_part = jax.nn.sigmoid(pre_act)
    hidden = pre_act * sigmoid_part
    slope_first = sigmoid_part * (1.0 + pre_act * (1.0 - sigmoid_part))
    slope_second = (
        sigmoid_part * (1.0 - sigmoid_part) * (2.0 + pre_act * (1.0 - 2.0 * sigmoid_part))
    )
    value_float = value_row.astype(jnp.float32)
    q_value = jnp.sum(hidden * value_float, axis=-1)
    tangent = (slope_first * value_float).astype(jnp.bfloat16)
    action_grad = lax.dot_general(
        tangent, weights, (((1,), (1,)), ((), ())), preferred_element_type=jnp.float32
    )
    grad_norm = jnp.sqrt(jnp.sum(action_grad * action_grad, axis=-1, keepdims=True) + EPS)
    unit_grad = action_grad / grad_norm
    return (hidden, slope_first, slope_second, q_value, tangent, unit_grad, grad_norm)


def weight_term(left, right):
    return lax.dot_general(
        left, right, (((0,), (0,)), ((), ())), preferred_element_type=jnp.float32
    )


def body(action, state_term, target, weight_a, value_w):
    members = weight_a.shape[0]
    pairs = members * lax.axis_size("member") * (members * lax.axis_size("member") - 1)
    stored = []
    for member_pos in range(members):
        gathered = lax.all_gather(weight_a[member_pos], "row", axis=0, tiled=True)
        results = forward_member(gathered, value_w[member_pos], state_term[member_pos], action)
        stored.append((gathered,) + results)
    unit_stack = jnp.stack([entry[6].astype(jnp.bfloat16) for entry in stored], axis=0)
    everyone = lax.all_gather(unit_stack, "member", axis=0, tiled=True)
    total = jnp.sum(everyone.astype(jnp.float32), axis=0)
    gram = jnp.einsum("mra,nra->rmn", everyone, everyone, preferred_element_type=jnp.float32)
    diagonal_sum = jnp.trace(gram, axis1=1, axis2=2)
    diversity = (jnp.sum(gram, axis=(1, 2)) - diagonal_sum) / pairs
    weight_grads = []
    value_grads = []
    state_grads = []
    for member_pos in range(members):
        weights, hidden, slope_first, slope_second, q_value, tangent, unit_grad, grad_norm = stored[
            member_pos
        ]
        dir_grad = 2.0 * ETA / pairs * (total - unit_stack[member_pos].astype(jnp.float32))
        along = jnp.sum(unit_grad * dir_grad, axis=-1, keepdims=True)
        cotangent = ((dir_grad - unit_grad * along) / grad_norm).astype(jnp.bfloat16)
        back_term = jnp.dot(cotangent, weights, preferred_element_type=jnp.float32)
        residue = (q_value - target)[:, None]
        value_float = value_w[member_pos].astype(jnp.float32)
        pre_grad = value_float * (slope_first * residue + slope_second * back_term)
        value_grads.append(jnp.sum(hidden * residue + slope_first * back_term, axis=0))
        pre_b = pre_grad.astype(jnp.bfloat16)
        state_grads.append(pre_b)
        left = jnp.concatenate([action, cotangent], axis=0)
        right = jnp.concatenate([pre_b, tangent], axis=0)
        summed = lax.psum_scatter(
            weight_term(left, right).astype(jnp.bfloat16), "row", scatter_dimension=0, tiled=True
        )
        weight_grads.append(summed)
    value_total = lax.psum(jnp.stack(value_grads, axis=0).astype(jnp.bfloat16), "row").astype(
        jnp.float32
    )
    return (jnp.stack(weight_grads, axis=0), value_total, jnp.stack(state_grads, axis=0), diversity)


def solution(mesh):
    in_specs = (
        P("row", None),
        P("member", "row", None),
        P("row"),
        P("member", "row", None),
        P("member", None),
    )
    out_specs = (P("member", "row", None), P("member", None), P("member", "row", None), P("row"))
    return jax.shard_map(body, mesh=mesh, in_specs=in_specs, out_specs=out_specs, check_vma=False)
```

profile of v0, /device:TPU:0, one launch (start us, length us, event | category | flops | bytes accessed | tf_op | source)
XLA Modules:
  0.0 579.9 jit_solution(1084699841644048765)
XLA Ops:
  7.2 0.0 all-gather.10.cloned.1.call-start
  7.2 2.3 fusion.46
  9.5 0.0 all-gather.10.cloned.1.call-update
  9.5 0.0 all-gather.8.cloned.1.call-start
  9.5 0.7 all-gather.8.cloned.1.call-update
  10.2 0.0 all-gather.6.cloned.1.call-start
  10.3 0.8 slice_convert_fusion.1
  11.1 75.1 %all-gather.10.cloned.1.call-done = bf16[1,1024,4096]{2,1,0:T(8,128)(2,1)} async-done(((bf16[1,64,4096]{2,1,0:T(8,128)(2,1)}), bf16[1,1024,4096]{2,1,0:T(8,128)(2,1)}) %all-gather.10.cloned.1.call-update) | async-done | bytes 8388624 | tf_op jit(solution)/shard_map/all_gather | solution.py:42
  86.2 0.0 copy-start.3
  86.2 10.1 %multiply_reduce_fusion = (f32[256]{0:T(256)S(1)}, bf16[256,4096]{1,0:T(8,128)(2,1)S(1)}, f32[256,4096]{1,0:T(8,128)}) fusion(f32[4096]{0:T(1024)S(1)} %bitcast.58, bf16[256,1024]{1,0:T(8,128)(2,1)} %param.5, bf16[1,1024,4096]{2,1,0:T(8,128)(2,1)} %all-gather.10.cloned.1.call-done, bf16[2,256,4096]{2,1,0:T(8,128)(2,1)} %param.6), kind=kOutput, calls=%fused_computation.46 | convolution fusion | flops 2162163456 | bytes 17318912 | tf_op jit(solution)/shard_map/dot_general | solution.py:11
  96.3 0.0 copy-start.7
  96.3 0.0 copy-done.3
  96.3 0.0 copy-start.4
  96.4 2.5 multiply_reduce_fusion.4
  98.8 0.0 copy-done.7
  98.8 61.0 %all-gather.8.cloned.1.call-done = bf16[1,1024,4096]{2,1,0:T(8,128)(2,1)} async-done(((bf16[1,64,4096]{2,1,0:T(8,128)(2,1)}), bf16[1,1024,4096]{2,1,0:T(8,128)(2,1)}) %all-gather.8.cloned.1.call-update) | async-done | bytes 8388624 | tf_op jit(solution)/shard_map/all_gather | solution.py:42
  159.8 0.0 copy-done.4
  159.8 0.0 copy-start.2
  159.8 9.7 %multiply_reduce_fusion.1 = (f32[256]{0:T(256)S(1)}, bf16[256,4096]{1,0:T(8,128)(2,1)S(1)}, f32[256,4096]{1,0:T(8,128)}) fusion(f32[4096]{0:T(1024)S(1)} %bitcast.56, bf16[256,1024]{1,0:T(8,128)(2,1)S(1)} %copy-done.4, bf16[1,1024,4096]{2,1,0:T(8,128)(2,1)} %all-gather.8.cloned.1.call-done, bf16[2,256,4096]{2,1,0:T(8,128)(2,1)} %param.6), kind=kOutput, calls=%fused_computation.47 | convolution fusion | flops 2162163456 | bytes 17318912 | tf_op jit(solution)/shard_map/dot_general | solution.py:11
  169.5 0.0 copy-start.5
  169.5 0.0 copy-done.2
  169.5 2.4 multiply_reduce_fusion.5
  172.0 0.0 copy-done.5
  172.0 0.0 copy-start.1
  172.0 0.3 convert_bitcast_fusion
  172.3 1.1 pad_maximum_fusion.5
  173.3 0.0 all-gather.6.cloned.1.call-update
  173.4 0.2 reduce-scatter.5.cloned.1.call-start
  173.6 0.0 copy-done.1
  173.6 166.1 %all-gather.6.cloned.1.call-done = bf16[16,256,1024]{2,1,0:T(8,128)(2,1)} async-done(((bf16[2,256,1024]{2,1,0:T(8,128)(2,1)}), bf16[16,256,1024]{2,1,0:T(8,128)(2,1)}) %all-gather.6.cloned.1.call-update) | async-done | bytes 8388624 | tf_op jit(solution)/shard_map/all_gather | solution.py:46
  339.8 5.5 convert_reduce_fusion
  345.3 0.0 copy-start.9
  345.3 0.5 multiply_reduce_fusion.3
  345.8 0.5 divide_convert_fusion.1
  346.4 1.1 copy-done.9
  347.5 0.0 copy-start.8
  347.5 7.4 %add_reduce_fusion = (bf16[4096]{0:T(1024)(128)(2,1)S(1)}, bf16[256,4096]{1,0:T(8,128)(2,1)S(1)}) fusion(f32[256]{0:T(256)S(1)} %get-tuple-element.23, f32[256,4096]{1,0:T(8,128)S(1)} %copy-done.9, f32[4096]{0:T(1024)S(1)} %bitcast.59, bf16[256,1024]{1,0:T(8,128)(2,1)S(1)} %get-tuple-element.17, bf16[1,1024,4096]{2,1,0:T(8,128)(2,1)} %all-gather.10.cloned.1.call-done), kind=kOutput, calls=%fused_computation.44 | convolution fusion | flops 2171596800 | bytes 15229952 | tf_op jit(solution)/shard_map/dot_general | solution.py:61
  354.9 0.0 copy-done.8
  354.9 6.8 %convolution_convert_fusion = bf16[1024,4096]{1,0:T(8,128)(2,1)} fusion(bf16[256,4096]{1,0:T(8,128)(2,1)S(1)} %copy-done.8, bf16[256,4096]{1,0:T(8,128)(2,1)S(1)} %get-tuple-element.11, bf16[256,1024]{1,0:T(8,128)(2,1)S(1)} %copy-done.4, bf16[256,1024]{1,0:T(8,128)(2,1)S(1)} %get-tuple-element.17), kind=kOutput, calls=%fused_computation.15 | convolution fusion | flops 4309647360 | bytes 13631488 | tf_op jit(solution)/shard_map/dot_general | solution.py:32
  361.7 0.0 reduce-scatter.5.cloned.1.call-update
  361.8 0.0 reduce-scatter.3.cloned.1.call-start
  361.8 0.0 copy-start.6
  361.8 10.1 %add_reduce_fusion.1 = (bf16[4096]{0:T(1024)(128)(2,1)S(1)}, bf16[256,4096]{1,0:T(8,128)(2,1)S(1)}) fusion(f32[256]{0:T(256)S(1)} %get-tuple-element.22, f32[256,4096]{1,0:T(8,128)} %get-tuple-element.27, f32[4096]{0:T(1024)S(1)} %bitcast.57, bf16[256,1024]{1,0:T(8,128)(2,1)S(1)} %get-tuple-element.16, bf16[1,1024,4096]{2,1,0:T(8,128)(2,1)} %all-gather.8.cloned.1.call-done), kind=kOutput, calls=%fused_computation.45 | convolution fusion | flops 2171596800 | bytes 15229952 | tf_op jit(solution)/shard_map/dot_general | solution.py:61
  371.9 0.0 copy-start
  371.9 1.4 copy-done
  373.3 0.0 copy-done.6
  373.3 6.7 %convolution_convert_fusion.1 = bf16[1024,4096]{1,0:T(8,128)(2,1)} fusion(bf16[256,4096]{1,0:T(8,128)(2,1)S(1)} %copy-done.6, bf16[256,4096]{1,0:T(8,128)(2,1)S(1)} %get-tuple-element.9, bf16[256,1024]{1,0:T(8,128)(2,1)S(1)} %copy-done.4, bf16[256,1024]{1,0:T(8,128)(2,1)S(1)} %get-tuple-element.16), kind=kOutput, calls=%fused_computation.16 | convolution fusion | flops 4309647360 | bytes 13631488 | tf_op jit(solution)/shard_map/dot_general | solution.py:32
  380.1 0.0 reduce-scatter.3.cloned.1.call-update
  380.2 69.7 %psum.7 = bf16[2,4096]{1,0:T(2,128)(2,1)S(1)} all-reduce(bf16[2,4096]{1,0:T(2,128)(2,1)S(1)} %pad_maximum_fusion.7), channel_id=1, replica_groups=mesh['member'=8,'row'=16] {'row'}, use_global_device_ids=true, to_apply=%region_11.12 | all-reduce | flops 8192 | bytes 32768 | tf_op jit(solution)/shard_map/psum | solution.py:74
  449.9 0.6 convert_element_type.78
  450.5 15.5 %select_reduce_fusion = (f32[256]{0:T(256)S(1)}, f32[256]{0:T(256)S(1)}) fusion(pred[16,16]{1,0:T(8,128)(4,1)S(1)} %iota_compare_fusion, bf16[16,256,1024]{2,1,0:T(8,128)(2,1)} %all-gather.6.cloned.1.call-done), kind=kOutput, calls=%fused_computation.54 | convolution fusion | flops 134413824 | bytes 8390912 | tf_op jit(solution)/shard_map/mra,nra->rmn/dot_general | solution.py:48
  466.0 0.6 subtract_multiply_fusion.6
  466.6 4.0 pad_maximum_fusion
  470.6 0.0 reduce-scatter.5.cloned.1.call-done
  470.6 100.5 %reduce-scatter.3.cloned.1.call-done = bf16[64,4096]{1,0:T(8,128)(2,1)} async-done(((bf16[1024,4096]{1,0:T(8,128)(2,1)}), bf16[64,4096]{1,0:T(8,128)(2,1)}) %reduce-scatter.3.cloned.1.call-update) | async-done | bytes 524304 | tf_op jit(solution)/shard_map/reduce_scatter | solution.py:70
  571.1 2.3 pad_maximum_fusion.6
  (7 shorter events, 0.1 us)
Async XLA Ops:
  7.2 79.0 %all-gather.10.cloned.1.call-start = ((), (), s32[]{:S(2)}) async-start(), calls=%async_computation.6 | async-start | bytes 8912896 | tf_op jit(solution)/shard_map/all_gather | solution.py:42
  9.5 150.3 %all-gather.8.cloned.1.call-start = ((), (), s32[]{:S(2)}) async-start(), calls=%async_computation.5 | async-start | bytes 8912896 | tf_op jit(solution)/shard_map/all_gather | solution.py:42
  10.2 329.5 %all-gather.6.cloned.1.call-start = ((), (), s32[]{:S(2)}) async-start(), calls=%async_computation.2 | async-start | bytes 9437184 | tf_op jit(solution)/shard_map/all_gather | solution.py:46
  86.2 10.2 %copy-start.3 = (bf16[1,1024,4096]{2,1,0:T(8,128)(2,1)S(1)}, bf16[1,1024,4096]{2,1,0:T(8,128)(2,1)}, u32[]{:S(2)}) copy-start(bf16[1,1024,4096]{2,1,0:T(8,128)(2,1)} %all-gather.10.cloned.1.call-done) | copy-start | bytes 25165828
  96.3 2.5 copy-start.7
  96.3 63.5 %copy-start.4 = (bf16[256,1024]{1,0:T(8,128)(2,1)S(1)}, bf16[256,1024]{1,0:T(8,128)(2,1)}, u32[]{:S(2)}) copy-start(bf16[256,1024]{1,0:T(8,128)(2,1)} %param.5) | copy-start | bytes 1572868
  159.8 9.7 %copy-start.2 = (bf16[1,1024,4096]{2,1,0:T(8,128)(2,1)S(1)}, bf16[1,1024,4096]{2,1,0:T(8,128)(2,1)}, u32[]{:S(2)}) copy-start(bf16[1,1024,4096]{2,1,0:T(8,128)(2,1)} %all-gather.8.cloned.1.call-done) | copy-start | bytes 25165828
  169.5 2.5 copy-start.5
  172.0 1.6 copy-start.1
  173.4 297.2 %reduce-scatter.5.cloned.1.call-start = ((), (), s32[]{:S(2)}) async-start(), calls=%async_computation.4 | async-start | bytes 8912896 | tf_op jit(solution)/shard_map/reduce_scatter | solution.py:70
  345.3 2.2 copy-start.9
  347.5 7.4 %copy-start.8 = (bf16[256,4096]{1,0:T(8,128)(2,1)S(1)}, bf16[256,4096]{1,0:T(8,128)(2,1)}, u32[]{:S(2)}) copy-start(bf16[256,4096]{1,0:T(8,128)(2,1)} %copy-done.7) | copy-start | bytes 6291460
  361.8 209.3 %reduce-scatter.3.cloned.1.call-start = ((), (), s32[]{:S(2)}) async-start(), calls=%async_computation.3 | async-start | bytes 8912896 | tf_op jit(solution)/shard_map/reduce_scatter | solution.py:70
  361.8 11.5 %copy-start.6 = (bf16[256,4096]{1,0:T(8,128)(2,1)S(1)}, bf16[256,4096]{1,0:T(8,128)(2,1)}, u32[]{:S(2)}) copy-start(bf16[256,4096]{1,0:T(8,128)(2,1)} %copy-done.5) | copy-start | bytes 6291460
  371.9 1.4 copy-start
Sparse Core Ops, SparseCore 0:
  11.0 75.1 all-gather.9
  89.2 70.5 all-gather.7
  173.5 166.2 all-gather.5
  361.9 103.6 reduce-scatter.4
  469.7 101.3 reduce-scatter.2
where the time goes:
time: 580 us
  waiting for transfers between devices  403 us (69%)
  matrix products  71.3 us (12%)
  blocking collectives  69.7 us (12%)
  other arithmetic  16.3 us (3%)
  between operations  13.9 us (2%)
    all_gather x1, waiting for transfers between devices, body(): everyone = lax.all_gather(unit_stack, 'member', axis=0, tiled=True)  166 us
    all_gather x2, waiting for transfers between devices, body(): gathered = lax.all_gather(weight_a[member_pos], 'row', axis=0, tiled=True)  136 us
    reduce_scatter x2, waiting for transfers between devices, body(): lax.psum_scatter(weight_term(left, right).astype(jnp.bfloat16), 'row', sc...  101 us
    psum x1, blocking collectives, body(): lax.psum(jnp.stack(value_grads, axis=0).astype(jnp.bfloat16), 'row')  69.7 us
    dot_general x2, matrix products, forward_member(): jnp.dot(action, weights, preferred_element_type=jnp.float32)  19.8 us
    dot_general x2, matrix products, body(): back_term = jnp.dot(cotangent, weights, preferred_element_type=jnp.float32)  17.5 us
    dot_general x1, matrix products, body(): jnp.einsum('mra,nra->rmn', everyone, everyone, preferred_element_type=jnp...  15.5 us
    dot_general x2, matrix products, weight_term(): lax.dot_general(left, right, (((0,), (0,)), ((), ())), preferred_element_...  13.6 us
  transfers between devices with their start and end apart: 5, of which 4 were waited for; matrix products, arithmetic and copies ran while one was open for 9% of the time, Pallas kernels for 0%

commit v1 on v0

v1 whole, which is shorter than its diff:
```python
import jax
import jax.numpy as jnp
from jax import lax
from jax.experimental import pallas as pl
from jax.experimental.pallas import tpu as pltpu
from jax.sharding import PartitionSpec as P

EPS = 1e-06
ETA = 5.0
MESH = pl.DeviceIdType.MESH
F32 = jnp.float32
BF16 = jnp.bfloat16

ACT = 1024
HID = 4096
ROWS = 256
LOCAL = 2
MEMBER_DEV = 8
PAIRS = 16 * 15
WIDTH = 256
PER_MEMBER = HID // WIDTH
BLOCKS = LOCAL * PER_MEMBER
PIECE = ROWS // MEMBER_DEV

SEND_AHEAD = 6
FORWARD_AHEAD = 4
SIBLING_AHEAD = 2
CORE_BEHIND = 1
SECOND_BEHIND = 3
LAST_BEHIND = 5


def x_first_in_scatter(block):
    return lax.rem(block * 9, 16) < 9


def wait_for(ref, sem):
    pltpu.make_async_copy(ref, ref, sem).wait()


def fold(value):
    out = value[:, 0:128]
    for pos in range(128, value.shape[1], 128):
        out = out + value[:, pos : pos + 128]
    return out


def wide(value, width):
    return jnp.concatenate([value] * (width // 128), axis=1)


def kernel(
    action_ref, state_hbm, target_ref, weight_hbm, value_ref,
    wgrad_hbm, vgrad_ref, sgrad_hbm, div_ref,
    wbuf, state, pre, grad, unit_b, cot, lhs, rhs, core_in, ring_in,
    piece_out, piece_in, total, square_out, square_in, value_w, q_acc, resid, rnorm, vsum, vin,
    load_sem, state_sem, x_sem, y_sem, second_sem, sib_sem, link_done, sib_done,
    core_sem, core_done, ring_sem, last_sem, ring_done, sgrad_sem, wgrad_sem,
    misc_sem,
):
    member = lax.axis_index("member")
    row = lax.axis_index("row")
    yhi = row // 8
    xpos = lax.rem(row // 2, 4)
    core = lax.rem(row, 2)
    oyhi = 1 - yhi
    ocore = 1 - core

    def at_row(yy, xx, cc):
        return (member, yy * 8 + xx * 2 + cc)

    sibling = at_row(yhi, xpos, ocore)
    across = at_row(oyhi, xpos, core)
    ring_x = [lax.rem(xpos + d, 4) for d in (1, 2, 3)]
    ring = [at_row(yhi, xx, core) for xx in ring_x]
    peers = [lax.rem(member + d, MEMBER_DEV) for d in range(1, MEMBER_DEV)]

    def send(src, dst, done, arrived, dev):
        pltpu.make_async_remote_copy(
            src_ref=src, dst_ref=dst, send_sem=done, recv_sem=arrived, device_id=dev, device_id_type=MESH
        ).start()

    barrier = pltpu.get_barrier_semaphore()
    everyone = [sibling, across] + ring + [(peer, row) for peer in peers]
    for dev in everyone:
        pl.semaphore_signal(barrier, inc=1, device_id=dev, device_id_type=MESH)

    def columns(block):
        return pl.ds(pl.multiple_of(lax.rem(block, PER_MEMBER) * WIDTH, WIDTH), WIDTH)

    def load_block(block, carry):
        m = block // PER_MEMBER
        pltpu.make_async_copy(
            weight_hbm.at[m, :, columns(block)], wbuf.at[block, yhi, xpos, core], load_sem.at[block]
        ).start()
        return carry

    lax.fori_loop(0, BLOCKS, load_block, 0)

    def load_state(block, carry):
        m = block // PER_MEMBER
        pltpu.make_async_copy(
            state_hbm.at[m, :, columns(block)], state.at[block], state_sem.at[block]
        ).start()
        return carry

    lax.fori_loop(0, BLOCKS, load_state, 0)

    for m in range(LOCAL):
        row_w = value_ref[m : m + 1, :].astype(F32)
        for pos in range(PER_MEMBER):
            value_w[m * PER_MEMBER + pos] = row_w[:, pos * WIDTH : (pos + 1) * WIDTH]
    grad[...] = jnp.zeros_like(grad)
    q_acc[...] = jnp.zeros_like(q_acc)
    for half in range(2):
        part = action_ref[half * 128 : (half + 1) * 128, :].astype(F32)
        lhs[:, half * 128 : (half + 1) * 128] = jnp.transpose(part).astype(BF16)

    pl.semaphore_wait(barrier, len(everyone))

    def first_send(b):
        wait_for(wbuf.at[b, yhi, xpos, core], load_sem.at[b])
        own = wbuf.at[b, yhi, xpos, core]
        for dev in ring:
            send(own, own, link_done.at[b], x_sem.at[b], dev)

        @pl.when(x_first_in_scatter(b))
        def _():
            send(own, own, link_done.at[b], y_sem.at[b], across)

    def forward(b):
        wait_for(wbuf.at[b, yhi, pl.ds(0, 3), core], x_sem.at[b])
        mine = wbuf.at[b, yhi, :, core]
        cross = x_first_in_scatter(b)

        @pl.when(jnp.logical_not(cross))
        def _():
            send(mine, mine, link_done.at[b], y_sem.at[b], across)

        send(mine, mine, sib_done.at[b], sib_sem.at[b], sibling)

        @pl.when(cross)
        def _():
            other = wbuf.at[b, oyhi, xpos, core]
            wait_for(other, y_sem.at[b])
            for dev in ring:
                send(other, other, link_done.at[b], second_sem.at[b], dev)

    def to_sibling(b):
        cross = x_first_in_scatter(b)

        @pl.when(cross)
        def _():
            wait_for(wbuf.at[b, oyhi, pl.ds(0, 3), core], second_sem.at[b])

        @pl.when(jnp.logical_not(cross))
        def _():
            wait_for(wbuf.at[b, oyhi, :, core], y_sem.at[b])

        theirs = wbuf.at[b, oyhi, :, core]
        send(theirs, theirs, sib_done.at[b], sib_sem.at[b], sibling)

    def compute_forward(b):
        m = b // PER_MEMBER
        wait_for(state.at[b], state_sem.at[b])
        wait_for(wbuf.at[b, :, :, ocore], sib_sem.at[b])
        weights = wbuf[b].reshape(ACT, WIDTH)
        pre[b] = state[b].astype(F32) + jnp.dot(action_ref[...], weights, preferred_element_type=F32)
        vw = value_w[b]
        step = 64
        for pos in range(0, ROWS, step):
            p = pre[b, pos : pos + step, :]
            sig = 0.5 + 0.5 * jnp.tanh(0.5 * p)
            hidden = p * sig
            slope = sig + hidden * (1.0 - sig)
            rhs[pos : pos + step, :] = (slope * vw).astype(BF16)
            q_acc[m, pos : pos + step, :] += fold(hidden * vw)
        grad[m] += lax.dot_general(
            rhs[0:ROWS, :], weights, (((1,), (1,)), ((), ())), preferred_element_type=F32
        )

    def forward_step(i, carry):
        t = i - SEND_AHEAD

        @pl.when(t + SEND_AHEAD < BLOCKS)
        def _():
            first_send(t + SEND_AHEAD)

        @pl.when(jnp.logical_and(t + FORWARD_AHEAD >= 0, t + FORWARD_AHEAD < BLOCKS))
        def _():
            forward(t + FORWARD_AHEAD)

        @pl.when(jnp.logical_and(t + SIBLING_AHEAD >= 0, t + SIBLING_AHEAD < BLOCKS))
        def _():
            to_sibling(t + SIBLING_AHEAD)

        @pl.when(t >= 0)
        def _():
            compute_forward(t)

        return carry

    lax.fori_loop(0, BLOCKS + SEND_AHEAD, forward_step, 0)

    def make_piece(k):
        rows = pl.ds(pl.multiple_of(k * PIECE, PIECE), PIECE)
        both = []
        squares = None
        for m in range(LOCAL):
            g = grad[m, rows, :]
            inv = 1.0 / jnp.sqrt(jnp.sum(g * g, axis=-1, keepdims=True) + EPS)
            u = g * inv
            ub = u.astype(BF16)
            grad[m, rows, :] = u
            unit_b[m, rows, :] = ub
            rnorm[m, rows, :] = jnp.broadcast_to(inv, (PIECE, 128))
            uf = ub.astype(F32)
            both.append(uf)
            sq = fold(uf * uf)
            squares = sq if squares is None else squares + sq
        square_out[rows, :] = squares
        return (both[0] + both[1]).astype(BF16)

    for peer in peers:
        piece_out[peer] = make_piece(peer)
        send(piece_out.at[peer], piece_in.at[member], misc_sem.at[0], misc_sem.at[1], (peer, row))
    piece_in[member] = make_piece(member)

    target_rows = jnp.transpose(jnp.broadcast_to(target_ref[...], (128, ROWS)))
    for m in range(LOCAL):
        q = jnp.sum(q_acc[m], axis=-1, keepdims=True)
        resid[m] = q - target_rows

    wait_for(piece_in.at[pl.ds(0, MEMBER_DEV - 1)], misc_sem.at[1])
    acc = piece_in[0].astype(F32)
    for k in range(1, MEMBER_DEV):
        acc = acc + piece_in[k].astype(F32)
    my_rows = pl.ds(pl.multiple_of(member * PIECE, PIECE), PIECE)
    total[my_rows, :] = acc.astype(BF16)
    for peer in peers:
        send(total.at[my_rows], total.at[my_rows], misc_sem.at[2], misc_sem.at[3], (peer, row))
    square_lane = jnp.sum(jnp.transpose(square_out[...]), axis=0, keepdims=True)
    square_in[member] = jnp.broadcast_to(square_lane, (8, ROWS))
    for peer in peers:
        send(square_in.at[member], square_in.at[member], misc_sem.at[4], misc_sem.at[5], (peer, row))
    wait_for(total.at[pl.ds(0, PIECE * (MEMBER_DEV - 1))], misc_sem.at[3])

    def make_cot(m):
        step = 64
        for pos in range(0, ROWS, step):
            u = grad[m, pos : pos + step, :]
            d = (2.0 * ETA / PAIRS) * (
                total[pos : pos + step, :].astype(F32) - unit_b[m, pos : pos + step, :].astype(F32)
            )
            along = jnp.sum(u * d, axis=-1, keepdims=True)
            c = (d - u * along) * wide(rnorm[m, pos : pos + step, :], ACT)
            cot[m, pos : pos + step, :] = c.astype(BF16)

    def place_cot(m):
        for half in range(2):
            part = cot[m, half * 128 : (half + 1) * 128, :].astype(F32)
            lhs[:, ROWS + half * 128 : ROWS + (half + 1) * 128] = jnp.transpose(part).astype(BF16)

    make_cot(0)
    place_cot(0)

    def compute_backward(b):
        m = b // PER_MEMBER
        weights = wbuf[b].reshape(ACT, WIDTH)
        back_all = jnp.dot(cot[m], weights, preferred_element_type=F32)
        vw = value_w[b]
        step = 64
        vacc = jnp.zeros((1, WIDTH), F32)
        for pos in range(0, ROWS, step):
            p = pre[b, pos : pos + step, :]
            back = back_all[pos : pos + step, :]
            res = wide(resid[m, pos : pos + step, :], WIDTH)
            sig = 0.5 + 0.5 * jnp.tanh(0.5 * p)
            rest = 1.0 - sig
            hidden = p * sig
            slope = sig + hidden * rest
            curve = sig * rest * (2.0 + p * (rest - sig))
            dpre = (vw * (slope * res + curve * back)).astype(BF16)
            vacc = vacc + jnp.sum(hidden * res + slope * back, axis=0, keepdims=True)
            rhs[pos : pos + step, :] = dpre
            state[b, pos : pos + step, :] = dpre
            rhs[ROWS + pos : ROWS + pos + step, :] = (slope * vw).astype(BF16)
        vsum[b] = vacc
        pltpu.make_async_copy(state.at[b], sgrad_hbm.at[m, :, columns(b)], sgrad_sem.at[b]).start()
        wait_for(wbuf.at[b, :, :, core], sib_done.at[b])
        wait_for(ring_in.at[b], link_done.at[b])
        part = jnp.dot(lhs[...], rhs[...], preferred_element_type=F32)
        wbuf[b] = part.astype(BF16).reshape(2, 4, 2, 64, WIDTH)
        send(wbuf.at[b, :, :, ocore], core_in.at[b], core_done.at[b], core_sem.at[b], sibling)

    def second_send(b):
        wait_for(core_in.at[b], core_sem.at[b])
        for yy in range(2):
            for xx in range(4):
                wbuf[b, yy, xx, core] = (
                    wbuf[b, yy, xx, core].astype(F32) + core_in[b, yy, xx].astype(F32)
                ).astype(BF16)
        x_first = x_first_in_scatter(b)

        @pl.when(x_first)
        def _():
            for d in range(3):
                send(
                    wbuf.at[b, :, ring_x[d], core], ring_in.at[b, pl.ds(2 * d, 2)],
                    ring_done.at[b], ring_sem.at[b], ring[d],
                )

        @pl.when(jnp.logical_not(x_first))
        def _():
            send(
                wbuf.at[b, oyhi, :, core], ring_in.at[b, pl.ds(0, 4)],
                ring_done.at[b], ring_sem.at[b], across,
            )

    def last_send(b):
        x_first = x_first_in_scatter(b)

        @pl.when(x_first)
        def _():
            wait_for(ring_in.at[b, pl.ds(0, 6)], ring_sem.at[b])
            for yy in range(2):
                s = wbuf[b, yy, xpos, core].astype(F32)
                for d in range(3):
                    s = s + ring_in[b, 2 * d + yy].astype(F32)
                wbuf[b, yy, xpos, core] = s.astype(BF16)
            send(
                wbuf.at[b, oyhi, xpos, core], ring_in.at[b, 6],
                ring_done.at[b], last_sem.at[b], across,
            )

        @pl.when(jnp.logical_not(x_first))
        def _():
            wait_for(ring_in.at[b, pl.ds(0, 4)], ring_sem.at[b])
            for xx in range(4):
                wbuf[b, yhi, xx, core] = (
                    wbuf[b, yhi, xx, core].astype(F32) + ring_in[b, xx].astype(F32)
                ).astype(BF16)
            for d in range(3):
                send(
                    wbuf.at[b, yhi, ring_x[d], core], ring_in.at[b, 4 + d],
                    ring_done.at[b], last_sem.at[b], ring[d],
                )

    def finish(b):
        m = b // PER_MEMBER
        x_first = x_first_in_scatter(b)

        @pl.when(x_first)
        def _():
            wait_for(ring_in.at[b, 6], last_sem.at[b])
            wbuf[b, yhi, xpos, core] = (
                wbuf[b, yhi, xpos, core].astype(F32) + ring_in[b, 6].astype(F32)
            ).astype(BF16)

        @pl.when(jnp.logical_not(x_first))
        def _():
            wait_for(ring_in.at[b, pl.ds(4, 3)], last_sem.at[b])
            s = wbuf[b, yhi, xpos, core].astype(F32)
            for d in range(3):
                s = s + ring_in[b, 4 + d].astype(F32)
            wbuf[b, yhi, xpos, core] = s.astype(BF16)

        pltpu.make_async_copy(
            wbuf.at[b, yhi, xpos, core], wgrad_hbm.at[m, :, columns(b)], wgrad_sem.at[b]
        ).start()

    def backward_step(t, carry):
        @pl.when(t == PER_MEMBER - 2)
        def _():
            make_cot(1)

        @pl.when(t == PER_MEMBER)
        def _():
            place_cot(1)

        @pl.when(t < BLOCKS)
        def _():
            compute_backward(t)

        @pl.when(t == BLOCKS)
        def _():
            send(vsum, vin.at[0], misc_sem.at[6], misc_sem.at[7], sibling)

        @pl.when(jnp.logical_and(t >= CORE_BEHIND, t - CORE_BEHIND < BLOCKS))
        def _():
            second_send(t - CORE_BEHIND)

        @pl.when(t == BLOCKS + 1)
        def _():
            wait_for(vsum, misc_sem.at[6])
            wait_for(vin.at[0], misc_sem.at[7])
            vsum[...] = vsum[...] + vin[0]
            send(vsum, vin.at[1], misc_sem.at[8], misc_sem.at[9], across)

        @pl.when(jnp.logical_and(t >= SECOND_BEHIND, t - SECOND_BEHIND < BLOCKS))
        def _():
            last_send(t - SECOND_BEHIND)

        @pl.when(t == BLOCKS + 3)
        def _():
            wait_for(vsum, misc_sem.at[8])
            wait_for(vin.at[1], misc_sem.at[9])
            vin[2 + xpos] = vsum[...] + vin[1]
            for dev in ring:
                send(vin.at[2 + xpos], vin.at[2 + xpos], misc_sem.at[10], misc_sem.at[11], dev)

        @pl.when(jnp.logical_and(t >= LAST_BEHIND, t - LAST_BEHIND < BLOCKS))
        def _():
            finish(t - LAST_BEHIND)

        return carry

    lax.fori_loop(0, BLOCKS + LAST_BEHIND, backward_step, 0)

    wait_for(square_in.at[pl.ds(0, MEMBER_DEV - 1)], misc_sem.at[5])
    tsq = []
    for pos in range(0, ROWS, 64):
        tf = total[pos : pos + 64, :].astype(F32)
        tsq.append(fold(tf * tf))
    cross_sum = jnp.sum(jnp.transpose(jnp.concatenate(tsq, axis=0)), axis=0, keepdims=True)
    squares = square_in[0]
    for k in range(1, MEMBER_DEV):
        squares = squares + square_in[k]
    div_ref[...] = (cross_sum - squares[0:1, :]) * (1.0 / PAIRS)

    wait_for(vin.at[pl.ds(2, 3)], misc_sem.at[11])
    for b in range(BLOCKS):
        m, pos = b // PER_MEMBER, b % PER_MEMBER
        vgrad_ref[m : m + 1, pos * WIDTH : (pos + 1) * WIDTH] = (vin[2, b] + vin[3, b]) + (vin[4, b] + vin[5, b])

    wait_for(piece_out.at[pl.ds(0, MEMBER_DEV - 1)], misc_sem.at[0])
    wait_for(total.at[pl.ds(0, PIECE * (MEMBER_DEV - 1))], misc_sem.at[2])
    wait_for(square_in.at[pl.ds(0, MEMBER_DEV - 1)], misc_sem.at[4])
    wait_for(vin.at[pl.ds(2, 3)], misc_sem.at[10])

    def drain(b, carry):
        m = b // PER_MEMBER
        wait_for(core_in.at[b], core_done.at[b])
        wait_for(ring_in.at[b], ring_done.at[b])
        wait_for(state.at[b], sgrad_sem.at[b])
        wait_for(wbuf.at[b, yhi, xpos, core], wgrad_sem.at[b])
        return carry

    lax.fori_loop(0, BLOCKS, drain, 0)


def body(action, state_term, target, weight_a, value_w):
    any_spec = pl.BlockSpec(memory_space=pl.ANY)
    vmem_spec = pl.BlockSpec(memory_space=pltpu.VMEM)
    dma = pltpu.SemaphoreType.DMA
    wgrad, vgrad, sgrad, div = pl.pallas_call(
        kernel,
        out_shape=(
            jax.ShapeDtypeStruct((LOCAL, 64, HID), BF16),
            jax.ShapeDtypeStruct((LOCAL, HID), F32),
            jax.ShapeDtypeStruct((LOCAL, ROWS, HID), BF16),
            jax.ShapeDtypeStruct((1, ROWS), F32),
        ),
        in_specs=[vmem_spec, any_spec, vmem_spec, any_spec, vmem_spec],
        out_specs=(any_spec, vmem_spec, any_spec, vmem_spec),
        scratch_shapes=[
            pltpu.VMEM((BLOCKS, 2, 4, 2, 64, WIDTH), BF16),
            pltpu.VMEM((BLOCKS, ROWS, WIDTH), BF16),
            pltpu.VMEM((BLOCKS, ROWS, WIDTH), F32),
            pltpu.VMEM((LOCAL, ROWS, ACT), F32),
            pltpu.VMEM((LOCAL, ROWS, ACT), BF16),
            pltpu.VMEM((LOCAL, ROWS, ACT), BF16),
            pltpu.VMEM((ACT, 2 * ROWS), BF16),
            pltpu.VMEM((2 * ROWS, WIDTH), BF16),
            pltpu.VMEM((BLOCKS, 2, 4, 64, WIDTH), BF16),
            pltpu.VMEM((BLOCKS, 7, 64, WIDTH), BF16),
            pltpu.VMEM((MEMBER_DEV, PIECE, ACT), BF16),
            pltpu.VMEM((MEMBER_DEV, PIECE, ACT), BF16),
            pltpu.VMEM((ROWS, ACT), BF16),
            pltpu.VMEM((ROWS, 128), F32),
            pltpu.VMEM((MEMBER_DEV, 8, ROWS), F32),
            pltpu.VMEM((BLOCKS, 1, WIDTH), F32),
            pltpu.VMEM((LOCAL, ROWS, 128), F32),
            pltpu.VMEM((LOCAL, ROWS, 128), F32),
            pltpu.VMEM((LOCAL, ROWS, 128), F32),
            pltpu.VMEM((BLOCKS, 1, WIDTH), F32),
            pltpu.VMEM((6, BLOCKS, 1, WIDTH), F32),
        ]
        + [dma((BLOCKS,)) for _ in range(15)]
        + [dma((12,))],
        compiler_params=pltpu.CompilerParams(
            collective_id=1, has_side_effects=True, vmem_limit_bytes=60 * 1024 * 1024
        ),
    )(action, state_term, target.reshape(1, ROWS), weight_a, value_w)
    return (wgrad, vgrad, sgrad, div.reshape(ROWS))


def solution(mesh):
    in_specs = (
        P("row", None),
        P("member", "row", None),
        P("row"),
        P("member", "row", None),
        P("member", None),
    )
    out_specs = (P("member", "row", None), P("member", None), P("member", "row", None), P("row"))
    return jax.shard_map(body, mesh=mesh, in_specs=in_specs, out_specs=out_specs, check_vma=False)
```

time: 580 us -> 209 us (0.36)
  waiting for transfers between devices: 403 us -> 0 us
  Pallas kernels: 0 us -> 199 us
  matrix products: 71.3 us -> 0 us
  blocking collectives: 69.7 us -> 0 us
  other arithmetic: 16.3 us -> 0 us
  between operations: 13.9 us -> 0.64 us
    all_gather x3 -> x0, waiting for transfers between devices: 302 us -> none  [the longest x1 166 us: body(): everyone = lax.all_gather(unit_stack, 'member', axis=0, tiled=True)]
    pallas_call x0 -> x1, Pallas kernels: none -> 199 us  [body(): pl.pallas_call(kernel, out_shape=(jax.ShapeDtypeStruct((LOCAL, 64, HID),...]
    reduce_scatter x2 -> x0, waiting for transfers between devices: 101 us -> none  [body(): lax.psum_scatter(weight_term(left, right).astype(jnp.bfloat16), 'row', sc...]
    dot_general x9 -> x0, matrix products: 71.3 us -> none  [the longest x2 19.8 us: forward_member(): jnp.dot(action, weights, preferred_element_type=jnp.float32)]
    psum x1 -> x0, blocking collectives: 69.7 us -> none  [body(): lax.psum(jnp.stack(value_grads, axis=0).astype(jnp.bfloat16), 'row')]
    another operation x5 -> x0, other arithmetic: 7.65 us -> none  [the longest x1 3.99 us: body(): jnp.stack(state_grads, axis=0)]
    unnamed x20 -> x6, local copies, waits for them, and re-layouts: 2.53 us -> 8.93 us
    reduce_sum x2 -> x0, other arithmetic: 6.05 us -> none  [the longest x1 5.54 us: body(): total = jnp.sum(everyone.astype(jnp.float32), axis=0)]
  transfers between devices with their start and end apart: 5 -> 0, of which waited for: 4 -> 0; matrix products, arithmetic and copies ran while one was open for 9% -> 0% of each run, Pallas kernels for 0% -> 0%
where the time goes in v1:
time: 209 us
  Pallas kernels  199 us (95%)
  local copies, waits for them, and re-layouts  8.93 us (4%)
    pallas_call x1, Pallas kernels, body(): pl.pallas_call(kernel, out_shape=(jax.ShapeDtypeStruct((LOCAL, 64, HID),...  199 us
    unnamed x6, local copies, waits for them, and re-layouts  8.93 us

profile of v1, /device:TPU:0, one launch (start us, length us, event | category | flops | bytes accessed | tf_op | source)
XLA Modules:
  0.0 209.0 jit_solution(11312217530731701165)
XLA Ops:
  0.6 199.4 %shard_map.84 = (bf16[2,64,4096]{2,1,0:T(8,128)(2,1)}, f32[2,4096]{1,0:T(2,128)}, bf16[2,256,4096]{2,1,0:T(8,128)(2,1)}, f32[1,256]{1,0:T(1,128)}) custom-call(bf16[256,1024]{1,0:T(8,128)(2,1)} %action_ref.1, bf16[2,256,4096]{2,1,0:T(8,128)(2,1)} %state_hbm.1, f32[1,256]{1,0:T(1,128)} %bitcast.2, bf16[2,64,4096]{2,1,0:T(8,128)(2,1)} %weight_hbm.1, ...), custom_call_target="tpu_custom_call" | custom-call | tf_op jit(solution)/shard_map/pallas_call | solution.py:456
  200.1 2.3 %copy.13 = bf16[2,64,4096]{2,1,0:T(8,128)(2,1)} copy(bf16[2,64,4096]{2,1,0:T(8,128)(2,1)} %get-tuple-element.16) | data formatting | bytes 2097152
  202.4 1.4 copy.14
  203.7 0.0 copy-start
  203.8 4.7 %copy.15 = bf16[2,256,4096]{2,1,0:T(8,128)(2,1)} copy(bf16[2,256,4096]{2,1,0:T(8,128)(2,1)} %get-tuple-element.18) | data formatting | bytes 8388608
  208.5 0.0 copy-done
  208.5 0.6 copy.16
Async XLA Ops:
  203.7 4.7 %copy-start = (f32[1,256]{1,0:T(1,128)S(1)}, f32[1,256]{1,0:T(1,128)}, u32[]{:S(2)}) copy-start(f32[1,256]{1,0:T(1,128)} %get-tuple-element.11) | copy-start | bytes 3076

commit v2 on v1

--- a/solution.py
+++ b/solution.py
@@ -21,13 +21,17 @@
 PER_MEMBER = HID // WIDTH
 BLOCKS = LOCAL * PER_MEMBER
 PIECE = ROWS // MEMBER_DEV
-
-SEND_AHEAD = 6
-FORWARD_AHEAD = 4
+GROUP = 8
+SGRAD_PARTS = 4
+
+SEND_AHEAD = 24
+FORWARD_AHEAD = 16
+THIRD_AHEAD = 9
 SIBLING_AHEAD = 2
 CORE_BEHIND = 1
-SECOND_BEHIND = 3
-LAST_BEHIND = 5
+SECOND_BEHIND = 5
+THIRD_BEHIND = 8
+LAST_BEHIND = 11
 
 
 def x_first_in_scatter(block):
@@ -54,8 +58,8 @@
     wgrad_hbm, vgrad_ref, sgrad_hbm, div_ref,
     wbuf, state, pre, grad, unit_b, cot, lhs, rhs, core_in, ring_in,
     piece_out, piece_in, total, square_out, square_in, value_w, q_acc, resid, rnorm, vsum, vin,
-    load_sem, state_sem, x_sem, y_sem, second_sem, sib_sem, link_done, sib_done,
-    core_sem, core_done, ring_sem, last_sem, ring_done, sgrad_sem, wgrad_sem,
+    load_sem, state_sem, link_done, sib_done, core_done, ring_done, sgrad_sem, wgrad_sem,
+    x_sem, y_sem, second_sem, sib_sem, core_sem, ring_sem, mid_sem, last_sem,
     misc_sem,
 ):
     member = lax.axis_index("member")
@@ -71,8 +75,12 @@
 
     sibling = at_row(yhi, xpos, ocore)
     across = at_row(oyhi, xpos, core)
-    ring_x = [lax.rem(xpos + d, 4) for d in (1, 2, 3)]
-    ring = [at_row(yhi, xx, core) for xx in ring_x]
+    xright, xfar, xleft = [lax.rem(xpos + d, 4) for d in (1, 2, 3)]
+    right = at_row(yhi, xright, core)
+    left = at_row(yhi, xleft, core)
+    pair_first = at_row(yhi, xpos + 1 - 2 * lax.rem(xpos, 2), core)
+    pair_second = at_row(yhi, 3 - xpos, core)
+    low, high = pl.ds(0, 32), pl.ds(32, 32)
     peers = [lax.rem(member + d, MEMBER_DEV) for d in range(1, MEMBER_DEV)]
 
     def send(src, dst, done, arrived, dev):
@@ -81,7 +89,7 @@
         ).start()
 
     barrier = pltpu.get_barrier_semaphore()
-    everyone = [sibling, across] + ring + [(peer, row) for peer in peers]
+    everyone = [sibling, across, right, left] + [(peer, row) for peer in peers]
     for dev in everyone:
         pl.semaphore_signal(barrier, inc=1, device_id=dev, device_id_type=MESH)
 
@@ -91,7 +99,7 @@
     def load_block(block, carry):
         m = block // PER_MEMBER
         pltpu.make_async_copy(
-            weight_hbm.at[m, :, columns(block)], wbuf.at[block, yhi, xpos, core], load_sem.at[block]
+            weight_hbm.at[m, :, columns(block)], wbuf.at[block, yhi, xpos, core], load_sem.at[block // GROUP]
         ).start()
         return carry
 
@@ -100,7 +108,7 @@
     def load_state(block, carry):
         m = block // PER_MEMBER
         pltpu.make_async_copy(
-            state_hbm.at[m, :, columns(block)], state.at[block], state_sem.at[block]
+            state_hbm.at[m, :, columns(block)], state.at[block], state_sem.at[block // GROUP]
         ).start()
         return carry
 
@@ -119,50 +127,81 @@
     pl.semaphore_wait(barrier, len(everyone))
 
     def first_send(b):
-        wait_for(wbuf.at[b, yhi, xpos, core], load_sem.at[b])
         own = wbuf.at[b, yhi, xpos, core]
-        for dev in ring:
-            send(own, own, link_done.at[b], x_sem.at[b], dev)
-
-        @pl.when(x_first_in_scatter(b))
-        def _():
-            send(own, own, link_done.at[b], y_sem.at[b], across)
-
-    def forward(b):
-        wait_for(wbuf.at[b, yhi, pl.ds(0, 3), core], x_sem.at[b])
-        mine = wbuf.at[b, yhi, :, core]
-        cross = x_first_in_scatter(b)
-
-        @pl.when(jnp.logical_not(cross))
-        def _():
-            send(mine, mine, link_done.at[b], y_sem.at[b], across)
-
-        send(mine, mine, sib_done.at[b], sib_sem.at[b], sibling)
-
-        @pl.when(cross)
-        def _():
-            other = wbuf.at[b, oyhi, xpos, core]
-            wait_for(other, y_sem.at[b])
-            for dev in ring:
-                send(other, other, link_done.at[b], second_sem.at[b], dev)
+
+        @pl.when(lax.rem(b, GROUP) == 0)
+        def _():
+            wait_for(wbuf.at[pl.ds(b, GROUP), yhi, xpos, core], load_sem.at[b // GROUP])
+
+        kind_a = x_first_in_scatter(b)
+
+        @pl.when(kind_a)
+        def _():
+            send(own, own, link_done, y_sem.at[b], across)
+
+        @pl.when(jnp.logical_not(kind_a))
+        def _():
+            send(own, own, link_done, x_sem.at[b], right)
+            send(own, own, link_done, x_sem.at[b], left)
+
+    def second_hop(b):
+        kind_a = x_first_in_scatter(b)
+
+        @pl.when(kind_a)
+        def _():
+            wait_for(wbuf.at[b, oyhi, xpos, core], y_sem.at[b])
+            both = wbuf.at[b, :, xpos, core]
+            send(both, both, link_done, x_sem.at[b], right)
+            send(both, both, link_done, x_sem.at[b], left)
+
+        @pl.when(jnp.logical_not(kind_a))
+        def _():
+            wait_for(wbuf.at[b, yhi, pl.ds(0, 2), core], x_sem.at[b])
+            one = wbuf.at[b, yhi, xleft, core, low]
+            send(one, one, link_done, second_sem.at[b], right)
+            two = wbuf.at[b, yhi, xright, core, high]
+            send(two, two, link_done, second_sem.at[b], left)
+
+    def third_hop(b):
+        kind_a = x_first_in_scatter(b)
+
+        @pl.when(kind_a)
+        def _():
+            wait_for(wbuf.at[b, :, pl.ds(0, 2), core], x_sem.at[b])
+            one = wbuf.at[b, :, xleft, core, low]
+            send(one, one, link_done, second_sem.at[b], right)
+            two = wbuf.at[b, :, xright, core, high]
+            send(two, two, link_done, second_sem.at[b], left)
+
+        @pl.when(jnp.logical_not(kind_a))
+        def _():
+            wait_for(wbuf.at[b, yhi, xfar, core], second_sem.at[b])
+            mine = wbuf.at[b, yhi, :, core]
+            send(mine, mine, link_done, y_sem.at[b], across)
+            send(mine, mine, sib_done, sib_sem.at[b], sibling)
 
     def to_sibling(b):
-        cross = x_first_in_scatter(b)
-
-        @pl.when(cross)
-        def _():
-            wait_for(wbuf.at[b, oyhi, pl.ds(0, 3), core], second_sem.at[b])
-
-        @pl.when(jnp.logical_not(cross))
-        def _():
-            wait_for(wbuf.at[b, oyhi, :, core], y_sem.at[b])
-
-        theirs = wbuf.at[b, oyhi, :, core]
-        send(theirs, theirs, sib_done.at[b], sib_sem.at[b], sibling)
+        kind_a = x_first_in_scatter(b)
+
+        @pl.when(kind_a)
+        def _():
+            wait_for(wbuf.at[b, :, xfar, core], second_sem.at[b])
+            full = wbuf.at[b, :, :, core]
+            send(full, full, sib_done, sib_sem.at[b], sibling)
+
+        @pl.when(jnp.logical_not(kind_a))
+        def _():
+            theirs = wbuf.at[b, oyhi, :, core]
+            wait_for(theirs, y_sem.at[b])
+            send(theirs, theirs, sib_done, sib_sem.at[b], sibling)
 
     def compute_forward(b):
         m = b // PER_MEMBER
-        wait_for(state.at[b], state_sem.at[b])
+
+        @pl.when(lax.rem(b, GROUP) == 0)
+        def _():
+            wait_for(state.at[pl.ds(b, GROUP)], state_sem.at[b // GROUP])
+
         wait_for(wbuf.at[b, :, :, ocore], sib_sem.at[b])
         weights = wbuf[b].reshape(ACT, WIDTH)
         pre[b] = state[b].astype(F32) + jnp.dot(action_ref[...], weights, preferred_element_type=F32)
@@ -188,7 +227,11 @@
 
         @pl.when(jnp.logical_and(t + FORWARD_AHEAD >= 0, t + FORWARD_AHEAD < BLOCKS))
         def _():
-            forward(t + FORWARD_AHEAD)
+            second_hop(t + FORWARD_AHEAD)
+
+        @pl.when(jnp.logical_and(t + THIRD_AHEAD >= 0, t + THIRD_AHEAD < BLOCKS))
+        def _():
+            third_hop(t + THIRD_AHEAD)
 
         @pl.when(jnp.logical_and(t + SIBLING_AHEAD >= 0, t + SIBLING_AHEAD < BLOCKS))
         def _():
@@ -263,6 +306,8 @@
 
     make_cot(0)
     place_cot(0)
+    wait_for(ring_in, link_done)
+    wait_for(core_in, sib_done)
 
     def compute_backward(b):
         m = b // PER_MEMBER
@@ -286,12 +331,10 @@
             state[b, pos : pos + step, :] = dpre
             rhs[ROWS + pos : ROWS + pos + step, :] = (slope * vw).astype(BF16)
         vsum[b] = vacc
-        pltpu.make_async_copy(state.at[b], sgrad_hbm.at[m, :, columns(b)], sgrad_sem.at[b]).start()
-        wait_for(wbuf.at[b, :, :, core], sib_done.at[b])
-        wait_for(ring_in.at[b], link_done.at[b])
+        pltpu.make_async_copy(state.at[b], sgrad_hbm.at[m, :, columns(b)], sgrad_sem).start()
         part = jnp.dot(lhs[...], rhs[...], preferred_element_type=F32)
         wbuf[b] = part.astype(BF16).reshape(2, 4, 2, 64, WIDTH)
-        send(wbuf.at[b, :, :, ocore], core_in.at[b], core_done.at[b], core_sem.at[b], sibling)
+        send(wbuf.at[b, :, :, ocore], core_in.at[b], core_done, core_sem.at[b], sibling)
 
     def second_send(b):
         wait_for(core_in.at[b], core_sem.at[b])
@@ -300,73 +343,82 @@
                 wbuf[b, yy, xx, core] = (
                     wbuf[b, yy, xx, core].astype(F32) + core_in[b, yy, xx].astype(F32)
                 ).astype(BF16)
-        x_first = x_first_in_scatter(b)
-
-        @pl.when(x_first)
-        def _():
-            for d in range(3):
-                send(
-                    wbuf.at[b, :, ring_x[d], core], ring_in.at[b, pl.ds(2 * d, 2)],
-                    ring_done.at[b], ring_sem.at[b], ring[d],
-                )
-
-        @pl.when(jnp.logical_not(x_first))
-        def _():
-            send(
-                wbuf.at[b, oyhi, :, core], ring_in.at[b, pl.ds(0, 4)],
-                ring_done.at[b], ring_sem.at[b], across,
-            )
-
-    def last_send(b):
-        x_first = x_first_in_scatter(b)
-
-        @pl.when(x_first)
-        def _():
-            wait_for(ring_in.at[b, pl.ds(0, 6)], ring_sem.at[b])
+        kind_a = x_first_in_scatter(b)
+
+        @pl.when(kind_a)
+        def _():
+            send(wbuf.at[b, :, xfar, core, low], ring_in.at[b, pl.ds(0, 2), low], ring_done, ring_sem.at[b], right)
+            send(wbuf.at[b, :, xfar, core, high], ring_in.at[b, pl.ds(0, 2), high], ring_done, ring_sem.at[b], left)
+
+        @pl.when(jnp.logical_not(kind_a))
+        def _():
+            send(wbuf.at[b, oyhi, :, core], ring_in.at[b, pl.ds(0, 4)], ring_done, ring_sem.at[b], across)
+
+    def add_in(b, yy, xx, parts):
+        s = wbuf[b, yy, xx, core].astype(F32)
+        for part in parts:
+            s = s + ring_in[b, part].astype(F32)
+        wbuf[b, yy, xx, core] = s.astype(BF16)
+
+    def add_half(b, yy, xx, part, rows):
+        wbuf[b, yy, xx, core, rows] = (
+            wbuf[b, yy, xx, core, rows].astype(F32) + ring_in[b, part, rows].astype(F32)
+        ).astype(BF16)
+
+    def third_send(b):
+        kind_a = x_first_in_scatter(b)
+
+        @pl.when(kind_a)
+        def _():
+            wait_for(ring_in.at[b, pl.ds(0, 2)], ring_sem.at[b])
             for yy in range(2):
-                s = wbuf[b, yy, xpos, core].astype(F32)
-                for d in range(3):
-                    s = s + ring_in[b, 2 * d + yy].astype(F32)
-                wbuf[b, yy, xpos, core] = s.astype(BF16)
-            send(
-                wbuf.at[b, oyhi, xpos, core], ring_in.at[b, 6],
-                ring_done.at[b], last_sem.at[b], across,
-            )
-
-        @pl.when(jnp.logical_not(x_first))
+                add_half(b, yy, xright, yy, low)
+                add_half(b, yy, xleft, yy, high)
+            send(wbuf.at[b, :, xright, core], ring_in.at[b, pl.ds(2, 2)], ring_done, mid_sem.at[b], right)
+            send(wbuf.at[b, :, xleft, core], ring_in.at[b, pl.ds(4, 2)], ring_done, mid_sem.at[b], left)
+
+        @pl.when(jnp.logical_not(kind_a))
         def _():
             wait_for(ring_in.at[b, pl.ds(0, 4)], ring_sem.at[b])
             for xx in range(4):
-                wbuf[b, yhi, xx, core] = (
-                    wbuf[b, yhi, xx, core].astype(F32) + ring_in[b, xx].astype(F32)
-                ).astype(BF16)
-            for d in range(3):
-                send(
-                    wbuf.at[b, yhi, ring_x[d], core], ring_in.at[b, 4 + d],
-                    ring_done.at[b], last_sem.at[b], ring[d],
-                )
+                add_in(b, yhi, xx, [xx])
+            send(wbuf.at[b, yhi, xfar, core, low], ring_in.at[b, 4, low], ring_done, mid_sem.at[b], right)
+            send(wbuf.at[b, yhi, xfar, core, high], ring_in.at[b, 4, high], ring_done, mid_sem.at[b], left)
+
+    def last_send(b):
+        kind_a = x_first_in_scatter(b)
+
+        @pl.when(kind_a)
+        def _():
+            wait_for(ring_in.at[b, pl.ds(2, 4)], mid_sem.at[b])
+            for yy in range(2):
+                add_in(b, yy, xpos, [2 + yy, 4 + yy])
+            send(wbuf.at[b, oyhi, xpos, core], ring_in.at[b, 6], ring_done, last_sem.at[b], across)
+
+        @pl.when(jnp.logical_not(kind_a))
+        def _():
+            wait_for(ring_in.at[b, 4], mid_sem.at[b])
+            add_half(b, yhi, xright, 4, low)
+            add_half(b, yhi, xleft, 4, high)
+            send(wbuf.at[b, yhi, xright, core], ring_in.at[b, 5], ring_done, last_sem.at[b], right)
+            send(wbuf.at[b, yhi, xleft, core], ring_in.at[b, 6], ring_done, last_sem.at[b], left)
 
     def finish(b):
         m = b // PER_MEMBER
-        x_first = x_first_in_scatter(b)
-
-        @pl.when(x_first)
+        kind_a = x_first_in_scatter(b)
+
+        @pl.when(kind_a)
         def _():
             wait_for(ring_in.at[b, 6], last_sem.at[b])
-            wbuf[b, yhi, xpos, core] = (
-                wbuf[b, yhi, xpos, core].astype(F32) + ring_in[b, 6].astype(F32)
-            ).astype(BF16)
-
-        @pl.when(jnp.logical_not(x_first))
-        def _():
-            wait_for(ring_in.at[b, pl.ds(4, 3)], last_sem.at[b])
-            s = wbuf[b, yhi, xpos, core].astype(F32)
-            for d in range(3):
-                s = s + ring_in[b, 4 + d].astype(F32)
-            wbuf[b, yhi, xpos, core] = s.astype(BF16)
+            add_in(b, yhi, xpos, [6])
+
+        @pl.when(jnp.logical_not(kind_a))
+        def _():
+            wait_for(ring_in.at[b, pl.ds(5, 2)], last_sem.at[b])
+            add_in(b, yhi, xpos, [5, 6])
 
         pltpu.make_async_copy(
-            wbuf.at[b, yhi, xpos, core], wgrad_hbm.at[m, :, columns(b)], wgrad_sem.at[b]
+            wbuf.at[b, yhi, xpos, core], wgrad_hbm.at[m, :, columns(b)], wgrad_sem
         ).start()
 
     def backward_step(t, carry):
@@ -394,20 +446,28 @@
         def _():
             wait_for(vsum, misc_sem.at[6])
             wait_for(vin.at[0], misc_sem.at[7])
-            vsum[...] = vsum[...] + vin[0]
-            send(vsum, vin.at[1], misc_sem.at[8], misc_sem.at[9], across)
+            vin[1] = vsum[...] + vin[0]
+            send(vin.at[1], vin.at[2], misc_sem.at[8], misc_sem.at[9], across)
 
         @pl.when(jnp.logical_and(t >= SECOND_BEHIND, t - SECOND_BEHIND < BLOCKS))
         def _():
-            last_send(t - SECOND_BEHIND)
-
-        @pl.when(t == BLOCKS + 3)
-        def _():
-            wait_for(vsum, misc_sem.at[8])
-            wait_for(vin.at[1], misc_sem.at[9])
-            vin[2 + xpos] = vsum[...] + vin[1]
-            for dev in ring:
-                send(vin.at[2 + xpos], vin.at[2 + xpos], misc_sem.at[10], misc_sem.at[11], dev)
+            third_send(t - SECOND_BEHIND)
+
+        @pl.when(t == BLOCKS + 2)
+        def _():
+            wait_for(vin.at[2], misc_sem.at[9])
+            vin[3] = vin[1] + vin[2]
+            send(vin.at[3], vin.at[4], misc_sem.at[10], misc_sem.at[11], pair_first)
+
+        @pl.when(jnp.logical_and(t >= THIRD_BEHIND, t - THIRD_BEHIND < BLOCKS))
+        def _():
+            last_send(t - THIRD_BEHIND)
+
+        @pl.when(t == BLOCKS + 4)
+        def _():
+            wait_for(vin.at[4], misc_sem.at[11])
+            vin[5] = vin[3] + vin[4]
+            send(vin.at[5], vin.at[6], misc_sem.at[12], misc_sem.at[13], pair_second)
 
         @pl.when(jnp.logical_and(t >= LAST_BEHIND, t - LAST_BEHIND < BLOCKS))
         def _():
@@ -428,25 +488,45 @@
         squares = squares + square_in[k]
     div_ref[...] = (cross_sum - squares[0:1, :]) * (1.0 / PAIRS)
 
-    wait_for(vin.at[pl.ds(2, 3)], misc_sem.at[11])
+    wait_for(vin.at[6], misc_sem.at[13])
     for b in range(BLOCKS):
         m, pos = b // PER_MEMBER, b % PER_MEMBER
-        vgrad_ref[m : m + 1, pos * WIDTH : (pos + 1) * WIDTH] = (vin[2, b] + vin[3, b]) + (vin[4, b] + vin[5, b])
+        vgrad_ref[m : m + 1, pos * WIDTH : (pos + 1) * WIDTH] = vin[5, b] + vin[6, b]
 
     wait_for(piece_out.at[pl.ds(0, MEMBER_DEV - 1)], misc_sem.at[0])
     wait_for(total.at[pl.ds(0, PIECE * (MEMBER_DEV - 1))], misc_sem.at[2])
     wait_for(square_in.at[pl.ds(0, MEMBER_DEV - 1)], misc_sem.at[4])
-    wait_for(vin.at[pl.ds(2, 3)], misc_sem.at[10])
-
-    def drain(b, carry):
-        m = b // PER_MEMBER
-        wait_for(core_in.at[b], core_done.at[b])
-        wait_for(ring_in.at[b], ring_done.at[b])
-        wait_for(state.at[b], sgrad_sem.at[b])
-        wait_for(wbuf.at[b, yhi, xpos, core], wgrad_sem.at[b])
-        return carry
-
-    lax.fori_loop(0, BLOCKS, drain, 0)
+    for pos in (8, 10, 12):
+        wait_for(vin.at[0], misc_sem.at[pos])
+
+    wait_for(core_in, core_done)
+    wait_for(ring_in, ring_done)
+    wait_for(state, sgrad_sem)
+    wait_for(wbuf.at[:, yhi, xpos, core], wgrad_sem)
+
+
+def hand_out(
+    wgrad, vgrad, sgrad, div, wgrad_out, vgrad_out, sgrad_out, div_out,
+    wgrad_buf, vgrad_buf, sgrad_buf, div_buf, in_sem, out_sem,
+):
+    steps = []
+    for m in range(LOCAL):
+        for part in range(SGRAD_PARTS):
+            rows = pl.ds(part * (ROWS // SGRAD_PARTS), ROWS // SGRAD_PARTS)
+            steps.append((sgrad.at[m, rows], sgrad_buf.at[m, rows], sgrad_out.at[m, rows]))
+    for m in range(LOCAL):
+        steps.append((wgrad.at[m], wgrad_buf.at[m], wgrad_out.at[m]))
+    steps.append((vgrad, vgrad_buf, vgrad_out))
+    steps.append((div, div_buf, div_out))
+    loads = [pltpu.make_async_copy(src, buf, in_sem.at[i]) for i, (src, buf, dst) in enumerate(steps)]
+    stores = [pltpu.make_async_copy(buf, dst, out_sem.at[i]) for i, (src, buf, dst) in enumerate(steps)]
+    for load in loads:
+        load.start()
+    for load, store in zip(loads, stores):
+        load.wait()
+        store.start()
+    for store in stores:
+        store.wait()
 
 
 def body(action, state_term, target, weight_a, value_w):
@@ -484,14 +564,25 @@
             pltpu.VMEM((LOCAL, ROWS, 128), F32),
             pltpu.VMEM((LOCAL, ROWS, 128), F32),
             pltpu.VMEM((BLOCKS, 1, WIDTH), F32),
-            pltpu.VMEM((6, BLOCKS, 1, WIDTH), F32),
+            pltpu.VMEM((7, BLOCKS, 1, WIDTH), F32),
         ]
-        + [dma((BLOCKS,)) for _ in range(15)]
-        + [dma((12,))],
+        + [dma((BLOCKS // GROUP,)) for _ in range(2)]
+        + [dma for _ in range(6)]
+        + [dma((BLOCKS,)) for _ in range(8)]
+        + [dma((14,))],
         compiler_params=pltpu.CompilerParams(
             collective_id=1, has_side_effects=True, vmem_limit_bytes=60 * 1024 * 1024
         ),
     )(action, state_term, target.reshape(1, ROWS), weight_a, value_w)
+    wgrad, vgrad, sgrad, div = pl.pallas_call(
+        hand_out,
+        out_shape=tuple(jax.ShapeDtypeStruct(x.shape, x.dtype) for x in (wgrad, vgrad, sgrad, div)),
+        in_specs=[any_spec] * 4,
+        out_specs=(any_spec,) * 4,
+        scratch_shapes=[pltpu.VMEM(x.shape, x.dtype) for x in (wgrad, vgrad, sgrad, div)]
+        + [dma((2 + LOCAL * (SGRAD_PARTS + 1),))] * 2,
+        compiler_params=pltpu.CompilerParams(vmem_limit_bytes=60 * 1024 * 1024),
+    )(wgrad, vgrad, sgrad, div)
     return (wgrad, vgrad, sgrad, div.reshape(ROWS))
 
 

time: 209 us -> 166 us (0.79)
  Pallas kernels: 199 us -> 165 us
  local copies, waits for them, and re-layouts: 8.93 us -> 0 us
    pallas_call x1, Pallas kernels: 199 us -> 161 us  [body(): pl.pallas_call(kernel, out_shape=(jax.ShapeDtypeStruct((LOCAL, 64, HID),...]
    unnamed x6 -> x0, local copies, waits for them, and re-layouts: 8.93 us -> none
    pallas_call x0 -> x1, Pallas kernels: none -> 4.75 us  [body(): pl.pallas_call(hand_out, out_shape=tuple((jax.ShapeDtypeStruct(x.shape, x...]
where the time goes in v2:
time: 166 us
  Pallas kernels  165 us (99%)
    pallas_call x1, Pallas kernels, body(): pl.pallas_call(kernel, out_shape=(jax.ShapeDtypeStruct((LOCAL, 64, HID),...  161 us
    pallas_call x1, Pallas kernels, body(): pl.pallas_call(hand_out, out_shape=tuple((jax.ShapeDtypeStruct(x.shape, x...  4.75 us

profile of v2, /device:TPU:0, one launch (start us, length us, event | category | flops | bytes accessed | tf_op | source)
XLA Modules:
  0.0 166.0 jit_solution(1759575377231977379)
XLA Ops:
  0.6 160.6 %shard_map.84 = (bf16[2,64,4096]{2,1,0:T(8,128)(2,1)}, f32[2,4096]{1,0:T(2,128)}, bf16[2,256,4096]{2,1,0:T(8,128)(2,1)}, f32[1,256]{1,0:T(1,128)}) custom-call(bf16[256,1024]{1,0:T(8,128)(2,1)} %action_ref.1, bf16[2,256,4096]{2,1,0:T(8,128)(2,1)} %state_hbm.1, f32[1,256]{1,0:T(1,128)} %bitcast.2, bf16[2,64,4096]{2,1,0:T(8,128)(2,1)} %weight_hbm.1, ...), custom_call_target="tpu_custom_call" | custom-call | tf_op jit(solution)/shard_map/pallas_call | solution.py:536
  161.2 4.8 %shard_map.85 = (bf16[2,64,4096]{2,1,0:T(8,128)(2,1)}, f32[2,4096]{1,0:T(2,128)}, bf16[2,256,4096]{2,1,0:T(8,128)(2,1)}, f32[1,256]{1,0:T(1,128)}) custom-call(bf16[2,64,4096]{2,1,0:T(8,128)(2,1)} %get-tuple-element.12.wgrad, f32[2,4096]{1,0:T(2,128)} %get-tuple-element.13.vgrad, bf16[2,256,4096]{2,1,0:T(8,128)(2,1)} %get-tuple-element.14.sgrad, ...), custom_call_target="tpu_custom_call" | custom-call | tf_op jit(solution)/shard_map/pallas_call | solution.py:577

commit v3 on v2

--- a/solution.py
+++ b/solution.py
@@ -22,16 +22,18 @@
 BLOCKS = LOCAL * PER_MEMBER
 PIECE = ROWS // MEMBER_DEV
 GROUP = 8
+HALF_PIECE = PIECE // 2
+HALF = ROWS // 2
 SGRAD_PARTS = 4
 
 SEND_AHEAD = 24
 FORWARD_AHEAD = 16
 THIRD_AHEAD = 9
 SIBLING_AHEAD = 2
-CORE_BEHIND = 1
-SECOND_BEHIND = 5
-THIRD_BEHIND = 8
-LAST_BEHIND = 11
+CORE_BEHIND = 2
+SECOND_BEHIND = 6
+THIRD_BEHIND = 16
+LAST_BEHIND = 31
 
 
 def x_first_in_scatter(block):
@@ -56,7 +58,7 @@
 def kernel(
     action_ref, state_hbm, target_ref, weight_hbm, value_ref,
     wgrad_hbm, vgrad_ref, sgrad_hbm, div_ref,
-    wbuf, state, pre, grad, unit_b, cot, lhs, rhs, core_in, ring_in,
+    wbuf, state, hidden, slope, curve, grad, unit_b, cot, lhs, rhs, core_in, ring_in,
     piece_out, piece_in, total, square_out, square_in, value_w, q_acc, resid, rnorm, vsum, vin,
     load_sem, state_sem, link_done, sib_done, core_done, ring_done, sgrad_sem, wgrad_sem,
     x_sem, y_sem, second_sem, sib_sem, core_sem, ring_sem, mid_sem, last_sem,
@@ -122,7 +124,9 @@
     q_acc[...] = jnp.zeros_like(q_acc)
     for half in range(2):
         part = action_ref[half * 128 : (half + 1) * 128, :].astype(F32)
-        lhs[:, half * 128 : (half + 1) * 128] = jnp.transpose(part).astype(BF16)
+        turned = jnp.transpose(part).astype(BF16)
+        for m in range(LOCAL):
+            lhs[m, :, half * ROWS : half * ROWS + HALF] = turned
 
     pl.semaphore_wait(barrier, len(everyone))
 
@@ -195,28 +199,54 @@
             wait_for(theirs, y_sem.at[b])
             send(theirs, theirs, sib_done, sib_sem.at[b], sibling)
 
-    def compute_forward(b):
+    def arrive(b):
+        @pl.when(lax.rem(b, GROUP) == 0)
+        def _():
+            wait_for(state.at[pl.ds(b, GROUP)], state_sem.at[b // GROUP])
+
+        wait_for(wbuf.at[b, :, :, ocore], sib_sem.at[b])
+
+    def forward_product(b):
+        return jnp.dot(action_ref[...], wbuf[b].reshape(ACT, WIDTH), preferred_element_type=F32)
+
+    def forward_elementwise(b, product):
         m = b // PER_MEMBER
-
-        @pl.when(lax.rem(b, GROUP) == 0)
-        def _():
-            wait_for(state.at[pl.ds(b, GROUP)], state_sem.at[b // GROUP])
-
-        wait_for(wbuf.at[b, :, :, ocore], sib_sem.at[b])
-        weights = wbuf[b].reshape(ACT, WIDTH)
-        pre[b] = state[b].astype(F32) + jnp.dot(action_ref[...], weights, preferred_element_type=F32)
         vw = value_w[b]
         step = 64
         for pos in range(0, ROWS, step):
-            p = pre[b, pos : pos + step, :]
+            rows = slice(pos, pos + step)
+            p = state[b, rows, :].astype(F32) + product[rows, :]
             sig = 0.5 + 0.5 * jnp.tanh(0.5 * p)
-            hidden = p * sig
-            slope = sig + hidden * (1.0 - sig)
-            rhs[pos : pos + step, :] = (slope * vw).astype(BF16)
-            q_acc[m, pos : pos + step, :] += fold(hidden * vw)
-        grad[m] += lax.dot_general(
-            rhs[0:ROWS, :], weights, (((1,), (1,)), ((), ())), preferred_element_type=F32
+            rest = 1.0 - sig
+            hid = p * sig
+            first = sig + hid * rest
+            state[b, rows, :] = (first * vw).astype(BF16)
+            slope[b, rows, :] = first.astype(BF16)
+            curve[b, rows, :] = (sig * rest * (2.0 + p * (rest - sig)) * vw).astype(BF16)
+            hidden[b, rows, :] = hid.astype(BF16)
+            q_acc[m, rows, :] += fold(hid * vw)
+
+    def gradient_product(b):
+        grad[b // PER_MEMBER] += lax.dot_general(
+            state[b], wbuf[b].reshape(ACT, WIDTH), (((1,), (1,)), ((), ())), preferred_element_type=F32
         )
+
+    def compute_forward(t):
+        @pl.when(t == 0)
+        def _():
+            arrive(t)
+            forward_elementwise(t, forward_product(t))
+
+        @pl.when(t > 0)
+        def _():
+            arrive(t)
+            product = forward_product(t)
+            gradient_product(t - 1)
+            forward_elementwise(t, product)
+
+        @pl.when(t == BLOCKS - 1)
+        def _():
+            gradient_product(t)
 
     def forward_step(i, carry):
         t = i - SEND_AHEAD
@@ -245,8 +275,8 @@
 
     lax.fori_loop(0, BLOCKS + SEND_AHEAD, forward_step, 0)
 
-    def make_piece(k):
-        rows = pl.ds(pl.multiple_of(k * PIECE, PIECE), PIECE)
+    def make_piece(k, half):
+        rows = pl.ds(pl.multiple_of(k * PIECE + half * HALF_PIECE, HALF_PIECE), HALF_PIECE)
         both = []
         squares = None
         for m in range(LOCAL):
@@ -256,7 +286,7 @@
             ub = u.astype(BF16)
             grad[m, rows, :] = u
             unit_b[m, rows, :] = ub
-            rnorm[m, rows, :] = jnp.broadcast_to(inv, (PIECE, 128))
+            rnorm[m, rows, :] = jnp.broadcast_to(inv, (HALF_PIECE, 128))
             uf = ub.astype(F32)
             both.append(uf)
             sq = fold(uf * uf)
@@ -264,24 +294,31 @@
         square_out[rows, :] = squares
         return (both[0] + both[1]).astype(BF16)
 
-    for peer in peers:
-        piece_out[peer] = make_piece(peer)
-        send(piece_out.at[peer], piece_in.at[member], misc_sem.at[0], misc_sem.at[1], (peer, row))
-    piece_in[member] = make_piece(member)
+    for half in range(2):
+        rows = pl.ds(half * HALF_PIECE, HALF_PIECE)
+        for peer in peers:
+            piece_out[peer, rows] = make_piece(peer, half)
+            send(
+                piece_out.at[peer, rows], piece_in.at[member, rows],
+                misc_sem.at[0], misc_sem.at[14 + half], (peer, row),
+            )
+        piece_in[member, rows] = make_piece(member, half)
 
     target_rows = jnp.transpose(jnp.broadcast_to(target_ref[...], (128, ROWS)))
     for m in range(LOCAL):
         q = jnp.sum(q_acc[m], axis=-1, keepdims=True)
         resid[m] = q - target_rows
 
-    wait_for(piece_in.at[pl.ds(0, MEMBER_DEV - 1)], misc_sem.at[1])
-    acc = piece_in[0].astype(F32)
-    for k in range(1, MEMBER_DEV):
-        acc = acc + piece_in[k].astype(F32)
-    my_rows = pl.ds(pl.multiple_of(member * PIECE, PIECE), PIECE)
-    total[my_rows, :] = acc.astype(BF16)
-    for peer in peers:
-        send(total.at[my_rows], total.at[my_rows], misc_sem.at[2], misc_sem.at[3], (peer, row))
+    for half in range(2):
+        rows = pl.ds(half * HALF_PIECE, HALF_PIECE)
+        wait_for(piece_in.at[pl.ds(0, MEMBER_DEV - 1), rows], misc_sem.at[14 + half])
+        acc = piece_in[0, rows].astype(F32)
+        for k in range(1, MEMBER_DEV):
+            acc = acc + piece_in[k, rows].astype(F32)
+        mine = pl.ds(pl.multiple_of(member * PIECE + half * HALF_PIECE, HALF_PIECE), HALF_PIECE)
+        total[mine, :] = acc.astype(BF16)
+        for peer in peers:
+            send(total.at[mine], total.at[mine], misc_sem.at[2], misc_sem.at[3], (peer, row))
     square_lane = jnp.sum(jnp.transpose(square_out[...]), axis=0, keepdims=True)
     square_in[member] = jnp.broadcast_to(square_lane, (8, ROWS))
     for peer in peers:
@@ -302,39 +339,73 @@
     def place_cot(m):
         for half in range(2):
             part = cot[m, half * 128 : (half + 1) * 128, :].astype(F32)
-            lhs[:, ROWS + half * 128 : ROWS + (half + 1) * 128] = jnp.transpose(part).astype(BF16)
+            lhs[m, :, half * ROWS + HALF : (half + 1) * ROWS] = jnp.transpose(part).astype(BF16)
 
     make_cot(0)
     place_cot(0)
     wait_for(ring_in, link_done)
     wait_for(core_in, sib_done)
 
-    def compute_backward(b):
+    def back_product(b):
+        return jnp.dot(cot[b // PER_MEMBER], wbuf[b].reshape(ACT, WIDTH), preferred_element_type=F32)
+
+    def partial_product(b):
         m = b // PER_MEMBER
-        weights = wbuf[b].reshape(ACT, WIDTH)
-        back_all = jnp.dot(cot[m], weights, preferred_element_type=F32)
-        vw = value_w[b]
+        slot = lax.rem(b, 2)
+        for q in range(4):
+            some = slice(q * 256, (q + 1) * 256)
+            part = jnp.dot(lhs[m, some, 0:ROWS], rhs[slot, 0:ROWS, :], preferred_element_type=F32)
+            part = part + jnp.dot(
+                lhs[m, some, ROWS : 2 * ROWS], rhs[slot, ROWS : 2 * ROWS, :], preferred_element_type=F32
+            )
+            wbuf[b, q // 2, 2 * (q % 2) : 2 * (q % 2) + 2] = part.astype(BF16).reshape(2, 2, 64, WIDTH)
+
+    def elementwise(b, back_all):
+        m = b // PER_MEMBER
+        slot = lax.rem(b, 2)
+        vacc = jnp.zeros((1, WIDTH), F32)
         step = 64
-        vacc = jnp.zeros((1, WIDTH), F32)
         for pos in range(0, ROWS, step):
-            p = pre[b, pos : pos + step, :]
-            back = back_all[pos : pos + step, :]
-            res = wide(resid[m, pos : pos + step, :], WIDTH)
-            sig = 0.5 + 0.5 * jnp.tanh(0.5 * p)
-            rest = 1.0 - sig
-            hidden = p * sig
-            slope = sig + hidden * rest
-            curve = sig * rest * (2.0 + p * (rest - sig))
-            dpre = (vw * (slope * res + curve * back)).astype(BF16)
-            vacc = vacc + jnp.sum(hidden * res + slope * back, axis=0, keepdims=True)
-            rhs[pos : pos + step, :] = dpre
-            state[b, pos : pos + step, :] = dpre
-            rhs[ROWS + pos : ROWS + pos + step, :] = (slope * vw).astype(BF16)
+            rows = slice(pos, pos + step)
+            at = pos + (pos // HALF) * HALF
+            back = back_all[rows, :]
+            res = wide(resid[m, rows, :], WIDTH)
+            tangent = state[b, rows, :]
+            dpre = (tangent.astype(F32) * res + curve[b, rows, :].astype(F32) * back).astype(BF16)
+            vacc = vacc + jnp.sum(
+                hidden[b, rows, :].astype(F32) * res + slope[b, rows, :].astype(F32) * back, axis=0, keepdims=True
+            )
+            rhs[slot, at : at + step, :] = dpre
+            rhs[slot, at + HALF : at + HALF + step, :] = tangent
+            state[b, rows, :] = dpre
         vsum[b] = vacc
-        pltpu.make_async_copy(state.at[b], sgrad_hbm.at[m, :, columns(b)], sgrad_sem).start()
-        part = jnp.dot(lhs[...], rhs[...], preferred_element_type=F32)
-        wbuf[b] = part.astype(BF16).reshape(2, 4, 2, 64, WIDTH)
+
+    def state_out(b):
+        pltpu.make_async_copy(
+            state.at[b], sgrad_hbm.at[b // PER_MEMBER, :, columns(b)], sgrad_sem
+        ).start()
+
+    def first_send_back(b):
         send(wbuf.at[b, :, :, ocore], core_in.at[b], core_done, core_sem.at[b], sibling)
+
+    def compute_backward(t):
+        @pl.when(t == 0)
+        def _():
+            elementwise(t, back_product(t))
+            state_out(t)
+
+        @pl.when(jnp.logical_and(t > 0, t < BLOCKS))
+        def _():
+            back_all = back_product(t)
+            partial_product(t - 1)
+            elementwise(t, back_all)
+            first_send_back(t - 1)
+            state_out(t)
+
+        @pl.when(t == BLOCKS)
+        def _():
+            partial_product(t - 1)
+            first_send_back(t - 1)
 
     def second_send(b):
         wait_for(core_in.at[b], core_sem.at[b])
@@ -425,16 +496,11 @@
         @pl.when(t == PER_MEMBER - 2)
         def _():
             make_cot(1)
-
-        @pl.when(t == PER_MEMBER)
-        def _():
             place_cot(1)
 
-        @pl.when(t < BLOCKS)
-        def _():
-            compute_backward(t)
-
-        @pl.when(t == BLOCKS)
+        compute_backward(t)
+
+        @pl.when(t == BLOCKS + 1)
         def _():
             send(vsum, vin.at[0], misc_sem.at[6], misc_sem.at[7], sibling)
 
@@ -442,7 +508,7 @@
         def _():
             second_send(t - CORE_BEHIND)
 
-        @pl.when(t == BLOCKS + 1)
+        @pl.when(t == BLOCKS + 2)
         def _():
             wait_for(vsum, misc_sem.at[6])
             wait_for(vin.at[0], misc_sem.at[7])
@@ -453,7 +519,7 @@
         def _():
             third_send(t - SECOND_BEHIND)
 
-        @pl.when(t == BLOCKS + 2)
+        @pl.when(t == BLOCKS + 3)
         def _():
             wait_for(vin.at[2], misc_sem.at[9])
             vin[3] = vin[1] + vin[2]
@@ -463,7 +529,7 @@
         def _():
             last_send(t - THIRD_BEHIND)
 
-        @pl.when(t == BLOCKS + 4)
+        @pl.when(t == BLOCKS + 5)
         def _():
             wait_for(vin.at[4], misc_sem.at[11])
             vin[5] = vin[3] + vin[4]
@@ -546,12 +612,14 @@
         scratch_shapes=[
             pltpu.VMEM((BLOCKS, 2, 4, 2, 64, WIDTH), BF16),
             pltpu.VMEM((BLOCKS, ROWS, WIDTH), BF16),
-            pltpu.VMEM((BLOCKS, ROWS, WIDTH), F32),
+            pltpu.VMEM((BLOCKS, ROWS, WIDTH), BF16),
+            pltpu.VMEM((BLOCKS, ROWS, WIDTH), BF16),
+            pltpu.VMEM((BLOCKS, ROWS, WIDTH), BF16),
             pltpu.VMEM((LOCAL, ROWS, ACT), F32),
             pltpu.VMEM((LOCAL, ROWS, ACT), BF16),
             pltpu.VMEM((LOCAL, ROWS, ACT), BF16),
-            pltpu.VMEM((ACT, 2 * ROWS), BF16),
-            pltpu.VMEM((2 * ROWS, WIDTH), BF16),
+            pltpu.VMEM((LOCAL, ACT, 2 * ROWS), BF16),
+            pltpu.VMEM((2, 2 * ROWS, WIDTH), BF16),
             pltpu.VMEM((BLOCKS, 2, 4, 64, WIDTH), BF16),
             pltpu.VMEM((BLOCKS, 7, 64, WIDTH), BF16),
             pltpu.VMEM((MEMBER_DEV, PIECE, ACT), BF16),
@@ -569,7 +637,7 @@
         + [dma((BLOCKS // GROUP,)) for _ in range(2)]
         + [dma for _ in range(6)]
         + [dma((BLOCKS,)) for _ in range(8)]
-        + [dma((14,))],
+        + [dma((16,))],
         compiler_params=pltpu.CompilerParams(
             collective_id=1, has_side_effects=True, vmem_limit_bytes=60 * 1024 * 1024
         ),

time: 166 us -> 158 us (0.952)
  Pallas kernels: 165 us -> 156 us
    pallas_call x1, Pallas kernels: 161 us -> 151 us  [body(): pl.pallas_call(kernel, out_shape=(jax.ShapeDtypeStruct((LOCAL, 64, HID),...]
where the time goes in v3:
time: 158 us; the launch traced here: 157 us
  Pallas kernels  156 us (99%)
    pallas_call x1, Pallas kernels, body(): pl.pallas_call(kernel, out_shape=(jax.ShapeDtypeStruct((LOCAL, 64, HID),...  151 us
    pallas_call x1, Pallas kernels, body(): pl.pallas_call(hand_out, out_shape=tuple((jax.ShapeDtypeStruct(x.shape, x...  4.75 us

profile of v3, /device:TPU:0, one launch (start us, length us, event | category | flops | bytes accessed | tf_op | source)
XLA Modules:
  0.0 156.6 jit_solution(14055522295936683838)
XLA Ops:
  0.6 151.2 %shard_map.84 = (bf16[2,64,4096]{2,1,0:T(8,128)(2,1)}, f32[2,4096]{1,0:T(2,128)}, bf16[2,256,4096]{2,1,0:T(8,128)(2,1)}, f32[1,256]{1,0:T(1,128)}) custom-call(bf16[256,1024]{1,0:T(8,128)(2,1)} %action_ref.1, bf16[2,256,4096]{2,1,0:T(8,128)(2,1)} %state_hbm.1, f32[1,256]{1,0:T(1,128)} %bitcast.2, bf16[2,64,4096]{2,1,0:T(8,128)(2,1)} %weight_hbm.1, ...), custom_call_target="tpu_custom_call" | custom-call | tf_op jit(solution)/shard_map/pallas_call | solution.py:602
  151.9 4.8 %shard_map.85 = (bf16[2,64,4096]{2,1,0:T(8,128)(2,1)}, f32[2,4096]{1,0:T(2,128)}, bf16[2,256,4096]{2,1,0:T(8,128)(2,1)}, f32[1,256]{1,0:T(1,128)}) custom-call(bf16[2,64,4096]{2,1,0:T(8,128)(2,1)} %get-tuple-element.12.wgrad, f32[2,4096]{1,0:T(2,128)} %get-tuple-element.13.vgrad, bf16[2,256,4096]{2,1,0:T(8,128)(2,1)} %get-tuple-element.14.sgrad, ...), custom_call_target="tpu_custom_call" | custom-call | tf_op jit(solution)/shard_map/pallas_call | solution.py:645

commit v4 on v3

--- a/solution.py
+++ b/solution.py
@@ -24,20 +24,53 @@
 GROUP = 8
 HALF_PIECE = PIECE // 2
 HALF = ROWS // 2
-SGRAD_PARTS = 4
-
-SEND_AHEAD = 24
-FORWARD_AHEAD = 16
-THIRD_AHEAD = 9
-SIBLING_AHEAD = 2
-CORE_BEHIND = 2
-SECOND_BEHIND = 6
-THIRD_BEHIND = 16
-LAST_BEHIND = 31
-
-
-def x_first_in_scatter(block):
-    return lax.rem(block * 9, 16) < 9
+
+GATHER_KINDS = "BABAABBBAAABBAAABABBAABAABBAAABA"
+SCATTER_KINDS = "AAABABABAAABABBBAAAAAABABBAABBAB"
+GATHER_STEPS = (
+    "3023233011001000312011220000000100000000000000000000",
+    "0000112201300220000102110110210210221000000000000000",
+    "0000000120031001310100100021030201031103000100000000",
+    "0000000000000212011011000030101002102211011211120000",
+)
+GATHER_LEAD = 20
+SCATTER_STEPS = (
+    "00001130111120111003021022100111011100100000",
+    "00000011100202021102000023010200001010201100",
+    "00000000000201011000112030000000110012212000",
+    "00000000000000000000000001010000200002330010",
+)
+PER_WORD = 13
+
+
+def is_a(kinds, block):
+    low, high = [
+        sum((letter == "A") << pos for pos, letter in enumerate(part)) for part in (kinds[:16], kinds[16:])
+    ]
+    return lax.rem(lax.shift_right_logical(jnp.where(block < 16, low, high), lax.rem(block, 16)), 2) == 1
+
+
+def count_at(digits, t):
+    words = [
+        sum(int(digit) << (2 * pos) for pos, digit in enumerate(digits[start : start + PER_WORD]))
+        for start in range(0, len(digits), PER_WORD)
+    ]
+    word = jnp.int32(words[0])
+    for pos in range(1, len(words)):
+        word = jnp.where(t // PER_WORD == pos, words[pos], word)
+    return lax.rem(lax.shift_right_logical(word, 2 * lax.rem(t, PER_WORD)), 4)
+
+
+def run_steps(steps, counts, done):
+    after = []
+    for step, count, first in zip(steps, counts, done):
+        def one(b, carry, step=step):
+            step(b)
+            return carry
+
+        lax.fori_loop(first, first + count, one, 0)
+        after.append(first + count)
+    return tuple(after)
 
 
 def wait_for(ref, sem):
@@ -57,11 +90,11 @@
 
 def kernel(
     action_ref, state_hbm, target_ref, weight_hbm, value_ref,
-    wgrad_hbm, vgrad_ref, sgrad_hbm, div_ref,
-    wbuf, state, hidden, slope, curve, grad, unit_b, cot, lhs, rhs, core_in, ring_in,
+    wgrad_ref, vgrad_ref, state, div_ref,
+    wbuf, hidden, slope, curve, grad, unit_b, cot, lhs, rhs, core_in, ring_in,
     piece_out, piece_in, total, square_out, square_in, value_w, q_acc, resid, rnorm, vsum, vin,
-    load_sem, state_sem, link_done, sib_done, core_done, ring_done, sgrad_sem, wgrad_sem,
-    x_sem, y_sem, second_sem, sib_sem, core_sem, ring_sem, mid_sem, last_sem,
+    load_sem, state_sem, link_done, sib_done, core_done, ring_done,
+    x_sem, y_sem, second_sem, sib_sem,
     misc_sem,
 ):
     member = lax.axis_index("member")
@@ -89,6 +122,8 @@
         pltpu.make_async_remote_copy(
             src_ref=src, dst_ref=dst, send_sem=done, recv_sem=arrived, device_id=dev, device_id_type=MESH
         ).start()
+
+    core_sem, ring_sem, mid_sem, last_sem = sib_sem, x_sem, second_sem, y_sem
 
     barrier = pltpu.get_barrier_semaphore()
     everyone = [sibling, across, right, left] + [(peer, row) for peer in peers]
@@ -137,7 +172,7 @@
         def _():
             wait_for(wbuf.at[pl.ds(b, GROUP), yhi, xpos, core], load_sem.at[b // GROUP])
 
-        kind_a = x_first_in_scatter(b)
+        kind_a = is_a(GATHER_KINDS, b)
 
         @pl.when(kind_a)
         def _():
@@ -149,7 +184,7 @@
             send(own, own, link_done, x_sem.at[b], left)
 
     def second_hop(b):
-        kind_a = x_first_in_scatter(b)
+        kind_a = is_a(GATHER_KINDS, b)
 
         @pl.when(kind_a)
         def _():
@@ -167,7 +202,7 @@
             send(two, two, link_done, second_sem.at[b], left)
 
     def third_hop(b):
-        kind_a = x_first_in_scatter(b)
+        kind_a = is_a(GATHER_KINDS, b)
 
         @pl.when(kind_a)
         def _():
@@ -185,7 +220,7 @@
             send(mine, mine, sib_done, sib_sem.at[b], sibling)
 
     def to_sibling(b):
-        kind_a = x_first_in_scatter(b)
+        kind_a = is_a(GATHER_KINDS, b)
 
         @pl.when(kind_a)
         def _():
@@ -248,32 +283,18 @@
         def _():
             gradient_product(t)
 
-    def forward_step(i, carry):
-        t = i - SEND_AHEAD
-
-        @pl.when(t + SEND_AHEAD < BLOCKS)
-        def _():
-            first_send(t + SEND_AHEAD)
-
-        @pl.when(jnp.logical_and(t + FORWARD_AHEAD >= 0, t + FORWARD_AHEAD < BLOCKS))
-        def _():
-            second_hop(t + FORWARD_AHEAD)
-
-        @pl.when(jnp.logical_and(t + THIRD_AHEAD >= 0, t + THIRD_AHEAD < BLOCKS))
-        def _():
-            third_hop(t + THIRD_AHEAD)
-
-        @pl.when(jnp.logical_and(t + SIBLING_AHEAD >= 0, t + SIBLING_AHEAD < BLOCKS))
-        def _():
-            to_sibling(t + SIBLING_AHEAD)
-
-        @pl.when(t >= 0)
-        def _():
-            compute_forward(t)
-
-        return carry
-
-    lax.fori_loop(0, BLOCKS + SEND_AHEAD, forward_step, 0)
+    def forward_round(i, done):
+        counts = [count_at(digits, i) for digits in GATHER_STEPS]
+        done = run_steps((first_send, second_hop, third_hop, to_sibling), counts, done)
+
+        @pl.when(i >= GATHER_LEAD)
+        def _():
+            compute_forward(i - GATHER_LEAD)
+
+        return done
+
+    zero = jnp.int32(0)
+    lax.fori_loop(0, BLOCKS + GATHER_LEAD, forward_round, (zero, zero, zero, zero))
 
     def make_piece(k, half):
         rows = pl.ds(pl.multiple_of(k * PIECE + half * HALF_PIECE, HALF_PIECE), HALF_PIECE)
@@ -380,11 +401,6 @@
             state[b, rows, :] = dpre
         vsum[b] = vacc
 
-    def state_out(b):
-        pltpu.make_async_copy(
-            state.at[b], sgrad_hbm.at[b // PER_MEMBER, :, columns(b)], sgrad_sem
-        ).start()
-
     def first_send_back(b):
         send(wbuf.at[b, :, :, ocore], core_in.at[b], core_done, core_sem.at[b], sibling)
 
@@ -392,7 +408,6 @@
         @pl.when(t == 0)
         def _():
             elementwise(t, back_product(t))
-            state_out(t)
 
         @pl.when(jnp.logical_and(t > 0, t < BLOCKS))
         def _():
@@ -400,7 +415,6 @@
             partial_product(t - 1)
             elementwise(t, back_all)
             first_send_back(t - 1)
-            state_out(t)
 
         @pl.when(t == BLOCKS)
         def _():
@@ -414,7 +428,7 @@
                 wbuf[b, yy, xx, core] = (
                     wbuf[b, yy, xx, core].astype(F32) + core_in[b, yy, xx].astype(F32)
                 ).astype(BF16)
-        kind_a = x_first_in_scatter(b)
+        kind_a = is_a(SCATTER_KINDS, b)
 
         @pl.when(kind_a)
         def _():
@@ -437,7 +451,7 @@
         ).astype(BF16)
 
     def third_send(b):
-        kind_a = x_first_in_scatter(b)
+        kind_a = is_a(SCATTER_KINDS, b)
 
         @pl.when(kind_a)
         def _():
@@ -457,7 +471,7 @@
             send(wbuf.at[b, yhi, xfar, core, high], ring_in.at[b, 4, high], ring_done, mid_sem.at[b], left)
 
     def last_send(b):
-        kind_a = x_first_in_scatter(b)
+        kind_a = is_a(SCATTER_KINDS, b)
 
         @pl.when(kind_a)
         def _():
@@ -475,24 +489,27 @@
             send(wbuf.at[b, yhi, xleft, core], ring_in.at[b, 6], ring_done, last_sem.at[b], left)
 
     def finish(b):
-        m = b // PER_MEMBER
-        kind_a = x_first_in_scatter(b)
+        kind_a = is_a(SCATTER_KINDS, b)
+
+        def store(parts):
+            out = wbuf[b, yhi, xpos, core].astype(F32)
+            for part in parts:
+                out = out + ring_in[b, part].astype(F32)
+            wgrad_ref[b] = out.astype(BF16)
 
         @pl.when(kind_a)
         def _():
             wait_for(ring_in.at[b, 6], last_sem.at[b])
-            add_in(b, yhi, xpos, [6])
+            store([6])
 
         @pl.when(jnp.logical_not(kind_a))
         def _():
             wait_for(ring_in.at[b, pl.ds(5, 2)], last_sem.at[b])
-            add_in(b, yhi, xpos, [5, 6])
-
-        pltpu.make_async_copy(
-            wbuf.at[b, yhi, xpos, core], wgrad_hbm.at[m, :, columns(b)], wgrad_sem
-        ).start()
-
-    def backward_step(t, carry):
+            store([5, 6])
+
+    rounds = len(SCATTER_STEPS[0])
+
+    def backward_round(t, done):
         @pl.when(t == PER_MEMBER - 2)
         def _():
             make_cot(1)
@@ -504,44 +521,32 @@
         def _():
             send(vsum, vin.at[0], misc_sem.at[6], misc_sem.at[7], sibling)
 
-        @pl.when(jnp.logical_and(t >= CORE_BEHIND, t - CORE_BEHIND < BLOCKS))
-        def _():
-            second_send(t - CORE_BEHIND)
-
-        @pl.when(t == BLOCKS + 2)
+        @pl.when(t == BLOCKS + 4)
         def _():
             wait_for(vsum, misc_sem.at[6])
             wait_for(vin.at[0], misc_sem.at[7])
             vin[1] = vsum[...] + vin[0]
             send(vin.at[1], vin.at[2], misc_sem.at[8], misc_sem.at[9], across)
 
-        @pl.when(jnp.logical_and(t >= SECOND_BEHIND, t - SECOND_BEHIND < BLOCKS))
-        def _():
-            third_send(t - SECOND_BEHIND)
-
-        @pl.when(t == BLOCKS + 3)
+        @pl.when(t == BLOCKS + 7)
         def _():
             wait_for(vin.at[2], misc_sem.at[9])
             vin[3] = vin[1] + vin[2]
             send(vin.at[3], vin.at[4], misc_sem.at[10], misc_sem.at[11], pair_first)
 
-        @pl.when(jnp.logical_and(t >= THIRD_BEHIND, t - THIRD_BEHIND < BLOCKS))
-        def _():
-            last_send(t - THIRD_BEHIND)
-
-        @pl.when(t == BLOCKS + 5)
+        @pl.when(t == rounds - 1)
         def _():
             wait_for(vin.at[4], misc_sem.at[11])
             vin[5] = vin[3] + vin[4]
             send(vin.at[5], vin.at[6], misc_sem.at[12], misc_sem.at[13], pair_second)
 
-        @pl.when(jnp.logical_and(t >= LAST_BEHIND, t - LAST_BEHIND < BLOCKS))
-        def _():
-            finish(t - LAST_BEHIND)
-
-        return carry
-
-    lax.fori_loop(0, BLOCKS + LAST_BEHIND, backward_step, 0)
+        counts = [
+            jnp.where(t == rounds - 1, BLOCKS - first, count_at(digits, t))
+            for digits, first in zip(SCATTER_STEPS, done)
+        ]
+        return run_steps((second_send, third_send, last_send, finish), counts, done)
+
+    lax.fori_loop(0, rounds, backward_round, (zero, zero, zero, zero))
 
     wait_for(square_in.at[pl.ds(0, MEMBER_DEV - 1)], misc_sem.at[5])
     tsq = []
@@ -567,32 +572,24 @@
 
     wait_for(core_in, core_done)
     wait_for(ring_in, ring_done)
-    wait_for(state, sgrad_sem)
-    wait_for(wbuf.at[:, yhi, xpos, core], wgrad_sem)
-
-
-def hand_out(
-    wgrad, vgrad, sgrad, div, wgrad_out, vgrad_out, sgrad_out, div_out,
-    wgrad_buf, vgrad_buf, sgrad_buf, div_buf, in_sem, out_sem,
-):
-    steps = []
-    for m in range(LOCAL):
-        for part in range(SGRAD_PARTS):
-            rows = pl.ds(part * (ROWS // SGRAD_PARTS), ROWS // SGRAD_PARTS)
-            steps.append((sgrad.at[m, rows], sgrad_buf.at[m, rows], sgrad_out.at[m, rows]))
-    for m in range(LOCAL):
-        steps.append((wgrad.at[m], wgrad_buf.at[m], wgrad_out.at[m]))
-    steps.append((vgrad, vgrad_buf, vgrad_out))
-    steps.append((div, div_buf, div_out))
-    loads = [pltpu.make_async_copy(src, buf, in_sem.at[i]) for i, (src, buf, dst) in enumerate(steps)]
-    stores = [pltpu.make_async_copy(buf, dst, out_sem.at[i]) for i, (src, buf, dst) in enumerate(steps)]
-    for load in loads:
-        load.start()
-    for load, store in zip(loads, stores):
-        load.wait()
-        store.start()
-    for store in stores:
-        store.wait()
+
+
+def hand_out(wgrad, vgrad, sgrad, div, wgrad_out, vgrad_out, sgrad_out, div_out, sem):
+    for b in range(BLOCKS):
+        m, pos = b // PER_MEMBER, b % PER_MEMBER
+        cols = pl.ds(pos * WIDTH, WIDTH)
+        pltpu.make_async_copy(sgrad.at[b], sgrad_out.at[m, :, cols], sem.at[0]).start()
+        pltpu.make_async_copy(wgrad.at[b], wgrad_out.at[m, :, cols], sem.at[1]).start()
+    small = [
+        pltpu.make_async_copy(vgrad, vgrad_out, sem.at[2]),
+        pltpu.make_async_copy(div, div_out, sem.at[3]),
+    ]
+    for one in small:
+        one.start()
+    for one in small:
+        one.wait()
+    wait_for(wgrad, sem.at[1])
+    wait_for(sgrad, sem.at[0])
 
 
 def body(action, state_term, target, weight_a, value_w):
@@ -602,16 +599,15 @@
     wgrad, vgrad, sgrad, div = pl.pallas_call(
         kernel,
         out_shape=(
-            jax.ShapeDtypeStruct((LOCAL, 64, HID), BF16),
-            jax.ShapeDtypeStruct((LOCAL, HID), F32),
-            jax.ShapeDtypeStruct((LOCAL, ROWS, HID), BF16),
-            jax.ShapeDtypeStruct((1, ROWS), F32),
+            pltpu.VMEM((BLOCKS, 64, WIDTH), BF16),
+            pltpu.VMEM((LOCAL, HID), F32),
+            pltpu.VMEM((BLOCKS, ROWS, WIDTH), BF16),
+            pltpu.VMEM((1, ROWS), F32),
         ),
         in_specs=[vmem_spec, any_spec, vmem_spec, any_spec, vmem_spec],
-        out_specs=(any_spec, vmem_spec, any_spec, vmem_spec),
+        out_specs=(vmem_spec,) * 4,
         scratch_shapes=[
             pltpu.VMEM((BLOCKS, 2, 4, 2, 64, WIDTH), BF16),
-            pltpu.VMEM((BLOCKS, ROWS, WIDTH), BF16),
             pltpu.VMEM((BLOCKS, ROWS, WIDTH), BF16),
             pltpu.VMEM((BLOCKS, ROWS, WIDTH), BF16),
             pltpu.VMEM((BLOCKS, ROWS, WIDTH), BF16),
@@ -635,21 +631,25 @@
             pltpu.VMEM((7, BLOCKS, 1, WIDTH), F32),
         ]
         + [dma((BLOCKS // GROUP,)) for _ in range(2)]
-        + [dma for _ in range(6)]
-        + [dma((BLOCKS,)) for _ in range(8)]
+        + [dma for _ in range(4)]
+        + [dma((BLOCKS,)) for _ in range(4)]
         + [dma((16,))],
         compiler_params=pltpu.CompilerParams(
-            collective_id=1, has_side_effects=True, vmem_limit_bytes=60 * 1024 * 1024
+            collective_id=1, has_side_effects=True, vmem_limit_bytes=56 * 1024 * 1024
         ),
     )(action, state_term, target.reshape(1, ROWS), weight_a, value_w)
     wgrad, vgrad, sgrad, div = pl.pallas_call(
         hand_out,
-        out_shape=tuple(jax.ShapeDtypeStruct(x.shape, x.dtype) for x in (wgrad, vgrad, sgrad, div)),
+        out_shape=(
+            jax.ShapeDtypeStruct((LOCAL, 64, HID), BF16),
+            jax.ShapeDtypeStruct((LOCAL, HID), F32),
+            jax.ShapeDtypeStruct((LOCAL, ROWS, HID), BF16),
+            jax.ShapeDtypeStruct((1, ROWS), F32),
+        ),
         in_specs=[any_spec] * 4,
         out_specs=(any_spec,) * 4,
-        scratch_shapes=[pltpu.VMEM(x.shape, x.dtype) for x in (wgrad, vgrad, sgrad, div)]
-        + [dma((2 + LOCAL * (SGRAD_PARTS + 1),))] * 2,
-        compiler_params=pltpu.CompilerParams(vmem_limit_bytes=60 * 1024 * 1024),
+        scratch_shapes=[dma((4,))],
+        compiler_params=pltpu.CompilerParams(vmem_limit_bytes=1024 * 1024),
     )(wgrad, vgrad, sgrad, div)
     return (wgrad, vgrad, sgrad, div.reshape(ROWS))
 

time: 158 us -> 151 us (0.956)
  Pallas kernels: 156 us -> 150 us
    pallas_call x2, Pallas kernels: 156 us -> 150 us  [the longest x1 148 us: body(): pl.pallas_call(kernel, out_shape=(pltpu.VMEM((BLOCKS, 64, WIDTH), BF16),...]
where the time goes in v4:
time: 151 us
  Pallas kernels  150 us (99%)
    pallas_call x1, Pallas kernels, body(): pl.pallas_call(kernel, out_shape=(pltpu.VMEM((BLOCKS, 64, WIDTH), BF16),...  148 us

profile of v4, /device:TPU:0, one launch (start us, length us, event | category | flops | bytes accessed | tf_op | source)
XLA Modules:
  0.0 151.1 jit_solution(3492909988140880158)
XLA Ops:
  0.6 148.2 %shard_map.84 = (bf16[32,64,256]{2,1,0:T(8,128)(2,1)S(1)}, f32[2,4096]{1,0:T(2,128)S(1)}, bf16[32,256,256]{2,1,0:T(8,128)(2,1)S(1)}, f32[1,256]{1,0:T(1,128)S(1)}) custom-call(bf16[256,1024]{1,0:T(8,128)(2,1)} %action_ref.1, bf16[2,256,4096]{2,1,0:T(8,128)(2,1)} %state_hbm.1, f32[1,256]{1,0:T(1,128)} %bitcast.2, bf16[2,64,4096]{2,1,0:T(8,128)(2,1)} %weight_hbm.1, ...), custom_call_target="tpu_custom_call" | custom-call | tf_op jit(solution)/shard_map/pallas_call | solution.py:599
  148.8 2.3 %shard_map.85 = (bf16[2,64,4096]{2,1,0:T(8,128)(2,1)}, f32[2,4096]{1,0:T(2,128)}, bf16[2,256,4096]{2,1,0:T(8,128)(2,1)}, f32[1,256]{1,0:T(1,128)}) custom-call(bf16[32,64,256]{2,1,0:T(8,128)(2,1)S(1)} %get-tuple-element.12.wgrad, f32[2,4096]{1,0:T(2,128)S(1)} %get-tuple-element.13.vgrad, bf16[32,256,256]{2,1,0:T(8,128)(2,1)S(1)} %get-tuple-element.14.sgrad, ...), custom_call_target="tpu_custom_call" | custom-call | tf_op jit(solution)/shard_map/pallas_call | solution.py:641

commit v5 on v4

--- a/solution.py
+++ b/solution.py
@@ -26,7 +26,7 @@
 HALF = ROWS // 2
 
 GATHER_KINDS = "BABAABBBAAABBAAABABBAABAABBAAABA"
-SCATTER_KINDS = "AAABABABAAABABBBAAAAAABABBAABBAB"
+SCATTER_KINDS = "ABABAABABBAABAABBAAAABBABABAABAB"
 GATHER_STEPS = (
     "3023233011001000312011220000000100000000000000000000",
     "0000112201300220000102110110210210221000000000000000",
@@ -35,10 +35,10 @@
 )
 GATHER_LEAD = 20
 SCATTER_STEPS = (
-    "00001130111120111003021022100111011100100000",
-    "00000011100202021102000023010200001010201100",
-    "00000000000201011000112030000000110012212000",
-    "00000000000000000000000001010000200002330010",
+    "00002021021102201031101201110112010110000000",
+    "00000001020300210302002301100020100210020010",
+    "00000000000012103011203001000100000003000020",
+    "00000000000000010010010100010000101200120210",
 )
 PER_WORD = 13
 
@@ -89,13 +89,13 @@
 
 
 def kernel(
-    action_ref, state_hbm, target_ref, weight_hbm, value_ref,
+    action_hbm, state_hbm, target_hbm, weight_hbm, value_hbm,
     wgrad_ref, vgrad_ref, state, div_ref,
     wbuf, hidden, slope, curve, grad, unit_b, cot, lhs, rhs, core_in, ring_in,
     piece_out, piece_in, total, square_out, square_in, value_w, q_acc, resid, rnorm, vsum, vin,
     load_sem, state_sem, link_done, sib_done, core_done, ring_done,
     x_sem, y_sem, second_sem, sib_sem,
-    misc_sem,
+    misc_sem, action_ref, target_ref, value_ref, small_sem,
 ):
     member = lax.axis_index("member")
     row = lax.axis_index("row")
@@ -141,6 +141,12 @@
         return carry
 
     lax.fori_loop(0, BLOCKS, load_block, 0)
+    small_loads = [
+        pltpu.make_async_copy(src, dst, small_sem.at[i])
+        for i, (src, dst) in enumerate(((value_hbm, value_ref), (action_hbm, action_ref), (target_hbm, target_ref)))
+    ]
+    for load in small_loads:
+        load.start()
 
     def load_state(block, carry):
         m = block // PER_MEMBER
@@ -151,6 +157,8 @@
 
     lax.fori_loop(0, BLOCKS, load_state, 0)
 
+    for load in small_loads:
+        load.wait()
     for m in range(LOCAL):
         row_w = value_ref[m : m + 1, :].astype(F32)
         for pos in range(PER_MEMBER):
@@ -207,6 +215,13 @@
         @pl.when(kind_a)
         def _():
             wait_for(wbuf.at[b, :, pl.ds(0, 2), core], x_sem.at[b])
+
+            @pl.when(b == BLOCKS - 1)
+            def _():
+                for xx in (xpos, xleft, xright):
+                    early = wbuf.at[b, :, xx, core]
+                    send(early, early, sib_done, sib_sem.at[b], sibling)
+
             one = wbuf.at[b, :, xleft, core, low]
             send(one, one, link_done, second_sem.at[b], right)
             two = wbuf.at[b, :, xright, core, high]
@@ -225,8 +240,16 @@
         @pl.when(kind_a)
         def _():
             wait_for(wbuf.at[b, :, xfar, core], second_sem.at[b])
-            full = wbuf.at[b, :, :, core]
-            send(full, full, sib_done, sib_sem.at[b], sibling)
+
+            @pl.when(b == BLOCKS - 1)
+            def _():
+                late = wbuf.at[b, :, xfar, core]
+                send(late, late, sib_done, sib_sem.at[b], sibling)
+
+            @pl.when(b < BLOCKS - 1)
+            def _():
+                full = wbuf.at[b, :, :, core]
+                send(full, full, sib_done, sib_sem.at[b], sibling)
 
         @pl.when(jnp.logical_not(kind_a))
         def _():
@@ -363,7 +386,6 @@
             lhs[m, :, half * ROWS + HALF : (half + 1) * ROWS] = jnp.transpose(part).astype(BF16)
 
     make_cot(0)
-    place_cot(0)
     wait_for(ring_in, link_done)
     wait_for(core_in, sib_done)
 
@@ -407,7 +429,9 @@
     def compute_backward(t):
         @pl.when(t == 0)
         def _():
-            elementwise(t, back_product(t))
+            back_all = back_product(t)
+            place_cot(0)
+            elementwise(t, back_all)
 
         @pl.when(jnp.logical_and(t > 0, t < BLOCKS))
         def _():
@@ -509,6 +533,18 @@
 
     rounds = len(SCATTER_STEPS[0])
 
+    def diversity():
+        wait_for(square_in.at[pl.ds(0, MEMBER_DEV - 1)], misc_sem.at[5])
+        tsq = []
+        for pos in range(0, ROWS, 64):
+            tf = total[pos : pos + 64, :].astype(F32)
+            tsq.append(fold(tf * tf))
+        cross_sum = jnp.sum(jnp.transpose(jnp.concatenate(tsq, axis=0)), axis=0, keepdims=True)
+        squares = square_in[0]
+        for k in range(1, MEMBER_DEV):
+            squares = squares + square_in[k]
+        div_ref[...] = (cross_sum - squares[0:1, :]) * (1.0 / PAIRS)
+
     def backward_round(t, done):
         @pl.when(t == PER_MEMBER - 2)
         def _():
@@ -516,6 +552,10 @@
             place_cot(1)
 
         compute_backward(t)
+
+        @pl.when(t == BLOCKS - 2)
+        def _():
+            diversity()
 
         @pl.when(t == BLOCKS + 1)
         def _():
@@ -547,17 +587,6 @@
         return run_steps((second_send, third_send, last_send, finish), counts, done)
 
     lax.fori_loop(0, rounds, backward_round, (zero, zero, zero, zero))
-
-    wait_for(square_in.at[pl.ds(0, MEMBER_DEV - 1)], misc_sem.at[5])
-    tsq = []
-    for pos in range(0, ROWS, 64):
-        tf = total[pos : pos + 64, :].astype(F32)
-        tsq.append(fold(tf * tf))
-    cross_sum = jnp.sum(jnp.transpose(jnp.concatenate(tsq, axis=0)), axis=0, keepdims=True)
-    squares = square_in[0]
-    for k in range(1, MEMBER_DEV):
-        squares = squares + square_in[k]
-    div_ref[...] = (cross_sum - squares[0:1, :]) * (1.0 / PAIRS)
 
     wait_for(vin.at[6], misc_sem.at[13])
     for b in range(BLOCKS):
@@ -604,7 +633,7 @@
             pltpu.VMEM((BLOCKS, ROWS, WIDTH), BF16),
             pltpu.VMEM((1, ROWS), F32),
         ),
-        in_specs=[vmem_spec, any_spec, vmem_spec, any_spec, vmem_spec],
+        in_specs=[any_spec] * 5,
         out_specs=(vmem_spec,) * 4,
         scratch_shapes=[
             pltpu.VMEM((BLOCKS, 2, 4, 2, 64, WIDTH), BF16),
@@ -633,7 +662,8 @@
         + [dma((BLOCKS // GROUP,)) for _ in range(2)]
         + [dma for _ in range(4)]
         + [dma((BLOCKS,)) for _ in range(4)]
-        + [dma((16,))],
+        + [dma((16,))]
+        + [pltpu.VMEM((ROWS, ACT), BF16), pltpu.VMEM((1, ROWS), F32), pltpu.VMEM((LOCAL, HID), BF16), dma((3,))],
         compiler_params=pltpu.CompilerParams(
             collective_id=1, has_side_effects=True, vmem_limit_bytes=56 * 1024 * 1024
         ),

time: 151 us -> 150 us (level)
    pallas_call x1, Pallas kernels: 148 us -> 147 us  [body(): pl.pallas_call(kernel, out_shape=(pltpu.VMEM((BLOCKS, 64, WIDTH), BF16),...]
where the time goes in v5:
time: 150 us
  Pallas kernels  149 us (99%)
    pallas_call x1, Pallas kernels, body(): pl.pallas_call(kernel, out_shape=(pltpu.VMEM((BLOCKS, 64, WIDTH), BF16),...  147 us

profile of v5, /device:TPU:0, one launch (start us, length us, event | category | flops | bytes accessed | tf_op | source)
XLA Modules:
  0.0 149.5 jit_solution(697020542294125196)
XLA Ops:
  0.6 146.6 %shard_map.84 = (bf16[32,64,256]{2,1,0:T(8,128)(2,1)S(1)}, f32[2,4096]{1,0:T(2,128)S(1)}, bf16[32,256,256]{2,1,0:T(8,128)(2,1)S(1)}, f32[1,256]{1,0:T(1,128)S(1)}) custom-call(bf16[256,1024]{1,0:T(8,128)(2,1)} %action_hbm.1, bf16[2,256,4096]{2,1,0:T(8,128)(2,1)} %state_hbm.1, f32[1,256]{1,0:T(1,128)} %bitcast.2, bf16[2,64,4096]{2,1,0:T(8,128)(2,1)} %weight_hbm.1, ...), custom_call_target="tpu_custom_call" | custom-call | tf_op jit(solution)/shard_map/pallas_call | solution.py:628
  147.2 2.3 %shard_map.85 = (bf16[2,64,4096]{2,1,0:T(8,128)(2,1)}, f32[2,4096]{1,0:T(2,128)}, bf16[2,256,4096]{2,1,0:T(8,128)(2,1)}, f32[1,256]{1,0:T(1,128)}) custom-call(bf16[32,64,256]{2,1,0:T(8,128)(2,1)S(1)} %get-tuple-element.12.wgrad, f32[2,4096]{1,0:T(2,128)S(1)} %get-tuple-element.13.vgrad, bf16[32,256,256]{2,1,0:T(8,128)(2,1)S(1)} %get-tuple-element.14.sgrad, ...), custom_call_target="tpu_custom_call" | custom-call | tf_op jit(solution)/shard_map/pallas_call | solution.py:671

commit v6 on v5

--- a/solution.py
+++ b/solution.py
@@ -35,10 +35,10 @@
 )
 GATHER_LEAD = 20
 SCATTER_STEPS = (
-    "00002021021102201031101201110112010110000000",
-    "00000001020300210302002301100020100210020010",
-    "00000000000012103011203001000100000003000020",
-    "00000000000000010010010100010000101200120210",
+    "00002021021102201031101201110112010110000000000",
+    "00000001020300210302002301100020100210020012000",
+    "00000000000012103011203001000100000003000023200",
+    "00000000000000010010010100010000101200120210000",
 )
 PER_WORD = 13
 
@@ -557,7 +557,7 @@
         def _():
             diversity()
 
-        @pl.when(t == BLOCKS + 1)
+        @pl.when(t == BLOCKS)
         def _():
             send(vsum, vin.at[0], misc_sem.at[6], misc_sem.at[7], sibling)
 
@@ -568,7 +568,7 @@
             vin[1] = vsum[...] + vin[0]
             send(vin.at[1], vin.at[2], misc_sem.at[8], misc_sem.at[9], across)
 
-        @pl.when(t == BLOCKS + 7)
+        @pl.when(t == BLOCKS + 11)
         def _():
             wait_for(vin.at[2], misc_sem.at[9])
             vin[3] = vin[1] + vin[2]

time: 150 us -> 147 us (0.980)
  Pallas kernels: 149 us -> 146 us
    pallas_call x1, Pallas kernels: 147 us -> 144 us  [body(): pl.pallas_call(kernel, out_shape=(pltpu.VMEM((BLOCKS, 64, WIDTH), BF16),...]
where the time goes in v6:
time: 147 us
  Pallas kernels  146 us (99%)
    pallas_call x1, Pallas kernels, body(): pl.pallas_call(kernel, out_shape=(pltpu.VMEM((BLOCKS, 64, WIDTH), BF16),...  144 us

profile of v6, /device:TPU:0, one launch (start us, length us, event | category | flops | bytes accessed | tf_op | source)
XLA Modules:
  0.0 147.1 jit_solution(13693965899348159285)
XLA Ops:
  0.6 144.1 %shard_map.84 = (bf16[32,64,256]{2,1,0:T(8,128)(2,1)S(1)}, f32[2,4096]{1,0:T(2,128)S(1)}, bf16[32,256,256]{2,1,0:T(8,128)(2,1)S(1)}, f32[1,256]{1,0:T(1,128)S(1)}) custom-call(bf16[256,1024]{1,0:T(8,128)(2,1)} %action_hbm.1, bf16[2,256,4096]{2,1,0:T(8,128)(2,1)} %state_hbm.1, f32[1,256]{1,0:T(1,128)} %bitcast.2, bf16[2,64,4096]{2,1,0:T(8,128)(2,1)} %weight_hbm.1, ...), custom_call_target="tpu_custom_call" | custom-call | tf_op jit(solution)/shard_map/pallas_call | solution.py:628
  144.8 2.3 %shard_map.85 = (bf16[2,64,4096]{2,1,0:T(8,128)(2,1)}, f32[2,4096]{1,0:T(2,128)}, bf16[2,256,4096]{2,1,0:T(8,128)(2,1)}, f32[1,256]{1,0:T(1,128)}) custom-call(bf16[32,64,256]{2,1,0:T(8,128)(2,1)S(1)} %get-tuple-element.12.wgrad, f32[2,4096]{1,0:T(2,128)S(1)} %get-tuple-element.13.vgrad, bf16[32,256,256]{2,1,0:T(8,128)(2,1)S(1)} %get-tuple-element.14.sgrad, ...), custom_call_target="tpu_custom_call" | custom-call | tf_op jit(solution)/shard_map/pallas_call | solution.py:671

commit v7 on v6

--- a/solution.py
+++ b/solution.py
@@ -25,13 +25,13 @@
 HALF_PIECE = PIECE // 2
 HALF = ROWS // 2
 
-GATHER_KINDS = "BABAABBBAAABBAAABABBAABAABBAAABA"
+GATHER_KINDS = "BABABBABABAAABABABBAABAABABAAAAA"
 SCATTER_KINDS = "ABABAABABBAABAABBAAAABBABABAABAB"
 GATHER_STEPS = (
-    "3023233011001000312011220000000100000000000000000000",
-    "0000112201300220000102110110210210221000000000000000",
-    "0000000120031001310100100021030201031103000100000000",
-    "0000000000000212011011000030101002102211011211120000",
+    "1133121113010121000020321011000000000000000000000000",
+    "0000011321001200101130101210123020000110000000000000",
+    "0000000000302200031101310011202001001101030101000000",
+    "0000000000000000101111011102022012102010121103111000",
 )
 GATHER_LEAD = 20
 SCATTER_STEPS = (
@@ -116,7 +116,7 @@
     pair_first = at_row(yhi, xpos + 1 - 2 * lax.rem(xpos, 2), core)
     pair_second = at_row(yhi, 3 - xpos, core)
     low, high = pl.ds(0, 32), pl.ds(32, 32)
-    peers = [lax.rem(member + d, MEMBER_DEV) for d in range(1, MEMBER_DEV)]
+    peers = [lax.rem(member + d, MEMBER_DEV) for d in (1, 7, 2, 6, 3, 5, 4)]
 
     def send(src, dst, done, arrived, dev):
         pltpu.make_async_remote_copy(

time: 147 us -> 147 us (level)
  no operation moved by 1% of the time
where the time goes in v7:
time: 147 us
  Pallas kernels  147 us (100%)
    pallas_call x1, Pallas kernels, body(): pl.pallas_call(kernel, out_shape=(pltpu.VMEM((BLOCKS, 64, WIDTH), BF16),...  144 us

profile of v7, /device:TPU:0, one launch (start us, length us, event | category | flops | bytes accessed | tf_op | source)
XLA Modules:
  0.0 147.3 jit_solution(15073101068931588392)
XLA Ops:
  0.6 144.3 %shard_map.84 = (bf16[32,64,256]{2,1,0:T(8,128)(2,1)S(1)}, f32[2,4096]{1,0:T(2,128)S(1)}, bf16[32,256,256]{2,1,0:T(8,128)(2,1)S(1)}, f32[1,256]{1,0:T(1,128)S(1)}) custom-call(bf16[256,1024]{1,0:T(8,128)(2,1)} %action_hbm.1, bf16[2,256,4096]{2,1,0:T(8,128)(2,1)} %state_hbm.1, f32[1,256]{1,0:T(1,128)} %bitcast.2, bf16[2,64,4096]{2,1,0:T(8,128)(2,1)} %weight_hbm.1, ...), custom_call_target="tpu_custom_call" | custom-call | tf_op jit(solution)/shard_map/pallas_call | solution.py:628
  144.9 2.3 %shard_map.85 = (bf16[2,64,4096]{2,1,0:T(8,128)(2,1)}, f32[2,4096]{1,0:T(2,128)}, bf16[2,256,4096]{2,1,0:T(8,128)(2,1)}, f32[1,256]{1,0:T(1,128)}) custom-call(bf16[32,64,256]{2,1,0:T(8,128)(2,1)S(1)} %get-tuple-element.12.wgrad, f32[2,4096]{1,0:T(2,128)S(1)} %get-tuple-element.13.vgrad, bf16[32,256,256]{2,1,0:T(8,128)(2,1)S(1)} %get-tuple-element.14.sgrad, ...), custom_call_target="tpu_custom_call" | custom-call | tf_op jit(solution)/shard_map/pallas_call | solution.py:671

commit v8 on v6

--- a/solution.py
+++ b/solution.py
@@ -437,8 +437,8 @@
         def _():
             back_all = back_product(t)
             partial_product(t - 1)
+            first_send_back(t - 1)
             elementwise(t, back_all)
-            first_send_back(t - 1)
 
         @pl.when(t == BLOCKS)
         def _():

time: 147 us -> 148 us (level)
  no operation moved by 1% of the time
where the time goes in v8:
time: 148 us
  Pallas kernels  147 us (99%)
    pallas_call x1, Pallas kernels, body(): pl.pallas_call(kernel, out_shape=(pltpu.VMEM((BLOCKS, 64, WIDTH), BF16),...  145 us

profile of v8, /device:TPU:0, one launch (start us, length us, event | category | flops | bytes accessed | tf_op | source)
XLA Modules:
  0.0 147.6 jit_solution(7727280369963703063)
XLA Ops:
  0.6 144.6 %shard_map.84 = (bf16[32,64,256]{2,1,0:T(8,128)(2,1)S(1)}, f32[2,4096]{1,0:T(2,128)S(1)}, bf16[32,256,256]{2,1,0:T(8,128)(2,1)S(1)}, f32[1,256]{1,0:T(1,128)S(1)}) custom-call(bf16[256,1024]{1,0:T(8,128)(2,1)} %action_hbm.1, bf16[2,256,4096]{2,1,0:T(8,128)(2,1)} %state_hbm.1, f32[1,256]{1,0:T(1,128)} %bitcast.2, bf16[2,64,4096]{2,1,0:T(8,128)(2,1)} %weight_hbm.1, ...), custom_call_target="tpu_custom_call" | custom-call | tf_op jit(solution)/shard_map/pallas_call | solution.py:628
  145.2 2.3 %shard_map.85 = (bf16[2,64,4096]{2,1,0:T(8,128)(2,1)}, f32[2,4096]{1,0:T(2,128)}, bf16[2,256,4096]{2,1,0:T(8,128)(2,1)}, f32[1,256]{1,0:T(1,128)}) custom-call(bf16[32,64,256]{2,1,0:T(8,128)(2,1)S(1)} %get-tuple-element.12.wgrad, f32[2,4096]{1,0:T(2,128)S(1)} %get-tuple-element.13.vgrad, bf16[32,256,256]{2,1,0:T(8,128)(2,1)S(1)} %get-tuple-element.14.sgrad, ...), custom_call_target="tpu_custom_call" | custom-call | tf_op jit(solution)/shard_map/pallas_call | solution.py:671
